TPU v7x, 256 devices: a whole 4x4x8 slice. The times are simulated.
256 devices in a mesh: seq: 32 (over z, x), req: 8 (over y, core).
Axes of the slice: x: 4, y: 4, z: 8, core: 2. Of those that a mesh axis runs over, the one named last changes fastest.
Arguments:
- tokens: bfloat16 [64, 4, 2048], P('req'), may hold values from -6 to 6
- lengths: int32 [64], P('req'), may hold values from 1 to 2044, as said below
- cache_keys: bfloat16 [64, 2048, 2048], P('req', 'seq'), may hold values from -120 to 120
- cache_values: bfloat16 [64, 2048, 2048], P('req', 'seq'), may hold values from -6 to 6
- norm1_gain: float32 [2048], replicated, may hold values from 0.5 to 1.5
- norm1_bias: float32 [2048], replicated, may hold values from -1.75 to 1.75
- w_query: bfloat16 [2048, 2048], P('req', 'seq'), may hold values from -0.125 to 0.125
- b_query: float32 [2048], P('seq'), may hold values from -3 to 3
- w_key: bfloat16 [2048, 2048], P('req', 'seq'), may hold values from -0.125 to 0.125
- b_key: float32 [2048], P('seq'), may hold values from -3 to 3
- w_value: bfloat16 [2048, 2048], P('req', 'seq'), may hold values from -0.125 to 0.125
- b_value: float32 [2048], P('seq'), may hold values from -3 to 3
- w_out: bfloat16 [2048, 2048], P('req', 'seq'), may hold values from -0.125 to 0.125
- b_out: float32 [2048], P('seq'), may hold values from -3 to 3
- norm2_gain: float32 [2048], replicated, may hold values from 0.5 to 1.5
- norm2_bias: float32 [2048], replicated, may hold values from -1.75 to 1.75
- w_up: bfloat16 [2048, 8192], P('req', 'seq'), may hold values from -0.125 to 0.125
- b_up: float32 [8192], P('seq'), may hold values from -3 to 3
- w_down: bfloat16 [8192, 2048], P('seq', 'req'), may hold values from -0.0625 to 0.0625
- b_down: float32 [2048], replicated, may hold values from -3 to 3
Outputs:
- hidden_out: bfloat16 [64, 4, 2048], P('req')
- new_keys: bfloat16 [64, 2048, 2048], P('req', 'seq')
- new_values: bfloat16 [64, 2048, 2048], P('req', 'seq')
Inputs may be any that keep to these rules, and one draw needn't show every extreme that they name: `lengths`: one request has exactly 2044 cached positions.
All inputs are finite; a program needn't handle non-finite values.
Results may differ from a plain program's by a relative error of at most 0.033.
Values may be sent and summed in bfloat16 or wider, within the bound.
A program may use at most 64 MiB of HBM per device.

v0:
```python
import jax
import jax.numpy as jnp
from jax import lax
from jax.sharding import PartitionSpec as P

HEADS = 16
HEAD = 128


def merged(x, axis, combine):
    everything = jax.tree.map(
        lambda part, kind: lax.all_gather(part.astype(kind), axis),
        x,
        (jnp.bfloat16, jnp.bfloat16, jnp.bfloat16),
    )

    def take(k):
        return jax.tree.map(lambda part, own: part[k].astype(own.dtype), everything, x)

    return lax.fori_loop(
        1, lax.axis_size(axis), lambda k, so_far: combine(so_far, take(k)), take(0)
    )


def layer_norm(values, gain, shift):
    center = values - jnp.mean(values, axis=-1, keepdims=True)
    spread = jnp.mean(center * center, axis=-1, keepdims=True)
    return center * lax.rsqrt(spread + 1e-05) * gain + shift


def combine(first, second):
    peak_a, total_a, part_a = first
    peak_b, total_b, part_b = second
    peak = jnp.maximum(peak_a, peak_b)
    scale_a = jnp.exp(peak_a - peak)
    scale_b = jnp.exp(peak_b - peak)
    total = total_a * scale_a + total_b * scale_b
    part = part_a * scale_a[..., None] + part_b * scale_b[..., None]
    return (peak, total, part)


def body(
    tokens,
    lengths,
    cache_keys,
    cache_values,
    norm1_gain,
    norm1_bias,
    w_query,
    b_query,
    w_key,
    b_key,
    w_value,
    b_value,
    w_out,
    b_out,
    norm2_gain,
    norm2_bias,
    w_up,
    b_up,
    w_down,
    b_down,
):
    group = tokens.shape[0]
    residual = tokens.astype(jnp.float32)
    normed = layer_norm(residual, norm1_gain, norm1_bias).astype(jnp.bfloat16)
    full_query, full_key, full_value, full_out, full_up = (
        lax.all_gather(w_query, "req", axis=0, tiled=True),
        lax.all_gather(w_key, "req", axis=0, tiled=True),
        lax.all_gather(w_value, "req", axis=0, tiled=True),
        lax.all_gather(w_out, "req", axis=0, tiled=True),
        lax.all_gather(w_up, "req", axis=0, tiled=True),
    )
    query_cols = (jnp.dot(normed, full_query, preferred_element_type=jnp.float32) + b_query).astype(
        jnp.bfloat16
    )
    key_cols = (jnp.dot(normed, full_key, preferred_element_type=jnp.float32) + b_key).astype(
        jnp.bfloat16
    )
    value_cols = (jnp.dot(normed, full_value, preferred_element_type=jnp.float32) + b_value).astype(
        jnp.bfloat16
    )
    query, key_rows, value_rows = (
        lax.all_gather(query_cols, "seq", axis=2, tiled=True),
        lax.all_gather(key_cols, "seq", axis=2, tiled=True),
        lax.all_gather(value_cols, "seq", axis=2, tiled=True),
    )
    steps, width = (query.shape[1], query.shape[2])
    slots = cache_keys.shape[1]
    position = lax.axis_index("seq") * slots + jnp.arange(slots, dtype=jnp.int32)
    new_keys = cache_keys
    new_values = cache_values
    for step in range(steps):
        hit = (position[None, :] == lengths[:, None] + step)[:, :, None]
        new_keys = jnp.where(hit, key_rows[:, step][:, None, :], new_keys)
        new_values = jnp.where(hit, value_rows[:, step][:, None, :], new_values)
    query_heads = query.reshape(group, steps, HEADS, HEAD)
    key_heads = new_keys.reshape(group, slots, HEADS, HEAD)
    value_heads = new_values.reshape(group, slots, HEADS, HEAD)
    scores = jnp.einsum(
        "rthd,rshd->rths", query_heads, key_heads, preferred_element_type=jnp.float32
    ) * HEAD ** (-0.5)
    limit = lengths[:, None] + jnp.arange(steps, dtype=jnp.int32)[None, :]
    valid = position[None, None, None, :] <= limit[:, :, None, None]
    masked = jnp.where(valid, scores, -1e30)
    peak = jnp.max(masked, axis=-1)
    expo = jnp.where(valid, jnp.exp(masked - peak[..., None]), 0.0)
    total = jnp.sum(expo, axis=-1)
    partial_value = jnp.einsum(
        "rths,rshd->rthd",
        expo.astype(jnp.bfloat16),
        value_heads,
        preferred_element_type=jnp.float32,
    )
    peak, total, partial_value = merged((peak, total, partial_value), "seq", combine)
    attn = (partial_value / total[..., None]).reshape(group, steps, width).astype(jnp.bfloat16)
    out_part = (jnp.dot(attn, full_out, preferred_element_type=jnp.float32) + b_out).astype(
        jnp.bfloat16
    )
    projected = lax.all_gather(out_part, "seq", axis=2, tiled=True)
    mid = residual + projected.astype(jnp.float32)
    normed2 = layer_norm(mid, norm2_gain, norm2_bias).astype(jnp.bfloat16)
    hidden = jax.nn.gelu(
        jnp.dot(normed2, full_up, preferred_element_type=jnp.float32) + b_up, approximate=False
    ).astype(jnp.bfloat16)
    feed = jnp.dot(
        hidden,
        lax.all_gather(w_down, "req", axis=1, tiled=True),
        preferred_element_type=jnp.float32,
    )
    summed = lax.psum(feed.astype(jnp.bfloat16), "seq").astype(jnp.float32)
    hidden_out = (mid + summed + b_down).astype(jnp.bfloat16)
    return (hidden_out, new_keys, new_values)


def solution(mesh):
    in_specs = (
        P("req", None, None),
        P("req"),
        P("req", "seq", None),
        P("req", "seq", None),
        P(),
        P(),
        P("req", "seq"),
        P("seq"),
        P("req", "seq"),
        P("seq"),
        P("req", "seq"),
        P("seq"),
        P("req", "seq"),
        P("seq"),
        P(),
        P(),
        P("req", "seq"),
        P("seq"),
        P("seq", "req"),
        P(),
    )
    out_specs = (P("req", None, None), P("req", "seq", None), P("req", "seq", None))
    return jax.shard_map(body, mesh=mesh, in_specs=in_specs, out_specs=out_specs, check_vma=False)
```

profile of v0, /device:TPU:2, one launch (start us, length us, event | category | flops | bytes accessed | tf_op | source)
XLA Modules:
  0.0 581.9 jit_solution(13199156575693389009)
XLA Ops:
  10.8 13.6 %all_gather.50 = bf16[2048,64]{0,1:T(8,128)(2,1)S(1)} all-gather(bf16[256,64]{0,1:T(8,128)(2,1)} %param.32), channel_id=1, replica_groups=mesh['seq'=32,'req'=8] {'req'}, dimensions={0}, use_global_device_ids=true | all-gather | bytes 294912 | tf_op jit(solution)/shard_map/all_gather | solution.py:70
  24.4 1.2 fusion.26
  25.7 54.4 %all_gather.51 = bf16[8,4,2048]{0,1,2:T(4,128)(2,1)S(1)} all-gather(bf16[8,4,64]{0,1,2:T(4,128)(2,1)S(1)} %copy.89), channel_id=1, replica_groups=mesh['seq'=32,'req'=8] {'seq'}, dimensions={2}, use_global_device_ids=true | all-gather | bytes 135168 | tf_op jit(solution)/shard_map/all_gather | solution.py:86
  80.1 3.8 fusion.133
  83.9 2.2 copy.105
  87.7 12.8 %all_gather.44 = bf16[2048,64]{0,1:T(8,128)(2,1)S(1)} all-gather(bf16[256,64]{0,1:T(8,128)(2,1)S(1)} %copy-done.3), channel_id=1, replica_groups=mesh['seq'=32,'req'=8] {'req'}, dimensions={0}, use_global_device_ids=true | all-gather | bytes 294912 | tf_op jit(solution)/shard_map/all_gather | solution.py:69
  100.9 50.0 %all_gather.45 = bf16[8,4,2048]{0,1,2:T(4,128)(2,1)S(1)} all-gather(bf16[8,4,64]{0,1,2:T(4,128)(2,1)S(1)} %copy.76), channel_id=1, replica_groups=mesh['seq'=32,'req'=8] {'seq'}, dimensions={2}, use_global_device_ids=true | all-gather | bytes 135168 | tf_op jit(solution)/shard_map/all_gather | solution.py:85
  151.0 3.8 fusion.134
  154.8 2.2 copy.101
  158.5 12.8 %all_gather.46 = bf16[2048,64]{0,1:T(8,128)(2,1)S(1)} all-gather(bf16[256,64]{0,1:T(8,128)(2,1)S(1)} %copy-done.4), channel_id=1, replica_groups=mesh['seq'=32,'req'=8] {'req'}, dimensions={0}, use_global_device_ids=true | all-gather | bytes 294912 | tf_op jit(solution)/shard_map/all_gather | solution.py:68
  171.7 50.1 %all_gather.47 = bf16[8,4,2048]{0,1,2:T(4,128)(2,1)S(1)} all-gather(bf16[8,4,64]{0,1,2:T(4,128)(2,1)S(1)} %copy.81), channel_id=1, replica_groups=mesh['seq'=32,'req'=8] {'seq'}, dimensions={2}, use_global_device_ids=true | all-gather | bytes 135168 | tf_op jit(solution)/shard_map/all_gather | solution.py:84
  223.0 2.9 select_select_fusion
  226.0 1.3 fusion.135
  231.1 47.5 %all-gather.1 = bf16[256,4,16]{2,1,0:T(4,128)(2,1)S(1)} all-gather(bf16[8,4,16]{2,1,0:T(4,128)(2,1)S(1)} %copy.88), channel_id=3, replica_groups=mesh['seq'=32,'req'=8] {'seq'}, dimensions={0}, use_global_device_ids=true | all-gather | bytes 33792 | tf_op jit(solution)/shard_map/all_gather | solution.py:12
  278.6 47.5 %all-gather = bf16[256,4,16]{2,1,0:T(4,128)(2,1)S(1)} all-gather(bf16[8,4,16]{2,1,0:T(4,128)(2,1)S(1)} %copy.86), channel_id=2, replica_groups=mesh['seq'=32,'req'=8] {'seq'}, dimensions={0}, use_global_device_ids=true | all-gather | bytes 33792 | tf_op jit(solution)/shard_map/all_gather | solution.py:12
  326.1 12.8 %all_gather.54 = bf16[2048,64]{0,1:T(8,128)(2,1)S(1)} all-gather(bf16[256,64]{0,1:T(8,128)(2,1)S(1)} %copy-done.5), channel_id=1, replica_groups=mesh['seq'=32,'req'=8] {'req'}, dimensions={0}, use_global_device_ids=true | all-gather | bytes 294912 | tf_op jit(solution)/shard_map/all_gather | solution.py:71
  339.9 38.4 %while.19 = (s32[]{:T(128)}, f32[8,4,16]{2,1,0:T(4,128)S(1)}, f32[8,4,16]{2,1,0:T(4,128)S(1)}, f32[8,4,16,128]{3,2,1,0:T(8,128)S(1)}, bf16[32,8,4,16]{3,2,1,0:T(...) while((s32[]{:T(128)}, f32[8,4,16]{2,1,0:T(4,128)S(1)}, ...), condition=%wide.region_5.6_spmd, body=%wide.region_4.5_spmd.sunk | while | flops 266245 | bytes 673943 | solution.py:20
  339.9 1.2 fusion.143
  341.2 1.2 fusion.143
  342.4 1.2 fusion.143
  343.6 1.2 fusion.143
  344.9 1.2 fusion.143
  346.1 1.2 fusion.143
  347.4 1.2 fusion.143
  348.6 1.2 fusion.143
  349.8 1.2 fusion.143
  351.1 1.2 fusion.143
  352.3 1.2 fusion.143
  353.5 1.2 fusion.143
  354.8 1.2 fusion.143
  356.0 1.2 fusion.143
  357.3 1.2 fusion.143
  358.5 1.2 fusion.143
  359.8 1.2 fusion.143
  361.0 1.2 fusion.143
  362.2 1.2 fusion.143
  363.5 1.2 fusion.143
  364.7 1.2 fusion.143
  365.9 1.2 fusion.143
  367.2 1.2 fusion.143
  369.6 1.2 fusion.143
  370.9 1.2 fusion.143
  375.8 1.2 fusion.143
  377.1 1.2 fusion.143
  378.8 50.4 %all_gather.55 = bf16[8,4,2048]{0,1,2:T(4,128)(2,1)S(1)} all-gather(bf16[8,4,64]{0,1,2:T(4,128)(2,1)S(1)} %copy.96), channel_id=1, replica_groups=mesh['seq'=32,'req'=8] {'seq'}, dimensions={2}, use_global_device_ids=true | all-gather | bytes 135168 | tf_op jit(solution)/shard_map/all_gather | solution.py:120
  430.9 1.6 fusion.94
  432.5 2.2 convolution_convert_fusion
  434.7 138.8 %all-reduce.2.cloned.1.call-done = bf16[8,4,2048]{2,0,1:T(8,128)(2,1)} async-done(((bf16[8,4,2048]{2,0,1:T(8,128)(2,1)}), bf16[8,4,2048]{2,0,1:T(8,128)(2,1)}) %all-reduce.2.cloned.1.call-update) | async-done | bytes 131088 | tf_op jit(solution)/shard_map/psum | solution.py:131
  (120 shorter events, 23.3 us)
Async XLA Ops:
  7.2 331.8 %all-gather.11.cloned.1.call-start = ((), (), s32[]{:S(2)}) async-start(), calls=%async_computation.3 | async-start | bytes 4325376 | tf_op jit(solution)/shard_map/all_gather | solution.py:12
  83.9 3.7 copy-start.3
  83.9 16.6 %copy-start = (bf16[8,4,2048]{2,1,0:T(4,128)(2,1)S(1)}, bf16[8,4,2048]{2,1,0:T(4,128)(2,1)}, u32[]{:S(2)}) copy-start(bf16[8,4,2048]{2,1,0:T(4,128)(2,1)} %param.22) | copy-start | bytes 393220
  83.9 16.6 %copy-start.11 = (f32[2048]{0:T(1024)S(1)}, f32[2048]{0:T(1024)}, u32[]{:S(2)}) copy-start(f32[2048]{0:T(1024)} %param.27) | copy-start | bytes 24580
  83.9 16.6 %copy-start.12 = (f32[2048]{0:T(1024)S(1)}, f32[2048]{0:T(1024)}, u32[]{:S(2)}) copy-start(f32[2048]{0:T(1024)} %param.26) | copy-start | bytes 24580
  83.9 16.6 %copy-start.13 = (f32[64]{0:T(128)S(1)}, f32[64]{0:T(128)}, u32[]{:S(2)}) copy-start(f32[64]{0:T(128)} %param.31) | copy-start | bytes 772
  154.8 3.7 copy-start.4
  154.8 16.5 %copy-start.14 = (f32[64]{0:T(128)S(1)}, f32[64]{0:T(128)}, u32[]{:S(2)}) copy-start(f32[64]{0:T(128)} %param.29) | copy-start | bytes 772
  171.7 51.2 %copy-start.9 = (s32[8]{0:T(128)S(1)}, s32[8]{0:T(128)}, u32[]{:S(2)}) copy-start(s32[8]{0:T(128)} %param.23) | copy-start | bytes 100
  226.0 2.0 copy-start.1
  226.0 2.0 copy-start.2
  227.2 98.8 %copy-start.5 = (bf16[256,64]{0,1:T(8,128)(2,1)S(1)}, bf16[256,64]{0,1:T(8,128)(2,1)}, u32[]{:S(2)}) copy-start(bf16[256,64]{0,1:T(8,128)(2,1)} %param.34) | copy-start | bytes 98308
  228.7 202.2 %all-gather.7.cloned.1.call-start = ((), (), s32[]{:S(2)}) async-start(), calls=%async_computation | async-start | bytes 1179648 | tf_op jit(solution)/shard_map/all_gather | solution.py:72
  229.5 203.0 %all-gather.9.cloned.1.call-start = ((), (), s32[]{:S(2)}) async-start(), calls=%async_computation.1 | async-start | bytes 1179648 | tf_op jit(solution)/shard_map/all_gather | solution.py:128
  230.2 343.4 %all-reduce.2.cloned.1.call-start = ((), (), s32[]{:S(2)}) async-start(), calls=%async_computation.2 | async-start | bytes 262144 | tf_op jit(solution)/shard_map/psum | solution.py:131
  339.9 38.6 %copy-start.15 = (f32[64]{0:T(128)S(1)}, f32[64]{0:T(128)}, u32[]{:S(2)}) copy-start(f32[64]{0:T(128)} %param.35) | copy-start | bytes 772
  378.8 52.1 %copy-start.6 = (f32[2048]{0:T(1024)S(1)}, f32[2048]{0:T(1024)}, u32[]{:S(2)}) copy-start(f32[2048]{0:T(1024)} %param.37) | copy-start | bytes 24580
  378.8 52.1 %copy-start.7 = (f32[2048]{0:T(1024)S(1)}, f32[2048]{0:T(1024)}, u32[]{:S(2)}) copy-start(f32[2048]{0:T(1024)} %param.36) | copy-start | bytes 24580
  378.8 52.1 %copy-start.10 = (f32[256]{0:T(256)S(1)}, f32[256]{0:T(256)}, u32[]{:S(2)}) copy-start(f32[256]{0:T(256)} %param.39) | copy-start | bytes 3076
  430.4 143.1 %copy-start.8 = (f32[2048]{0:T(1024)S(1)}, f32[2048]{0:T(1024)}, u32[]{:S(2)}) copy-start(f32[2048]{0:T(1024)} %param.41) | copy-start | bytes 24580
Sparse Core Ops, SparseCore 0:
  228.8 78.4 all-gather.10
  309.2 24.8 all-gather.6
  335.9 25.9 all-gather.8
  434.9 138.6 all-reduce.1
where the time goes:
time: 583 us; the launch traced here: 582 us
  blocking collectives  352 us (60%)
  waiting for transfers between devices  140 us (24%)
  other arithmetic  47.2 us (8%)
  local copies, waits for them, and re-layouts  19.5 us (3%)
  between operations  14.1 us (2%)
  matrix products  7.72 us (1%)
    psum x1, waiting for transfers between devices, body(): summed = lax.psum(feed.astype(jnp.bfloat16), 'seq').astype(jnp.float32)  139 us
    all_gather x2, blocking collectives, merged(): lax.all_gather(part.astype(kind), axis)  94.9 us
    all_gather x1, blocking collectives, body(): lax.all_gather(value_cols, 'seq', axis=2, tiled=True)  54.4 us
    all_gather x1, blocking collectives, body(): projected = lax.all_gather(out_part, 'seq', axis=2, tiled=True)  50.4 us
    all_gather x1, blocking collectives, body(): lax.all_gather(query_cols, 'seq', axis=2, tiled=True)  50.1 us
    all_gather x1, blocking collectives, body(): lax.all_gather(key_cols, 'seq', axis=2, tiled=True)  50 us
    add x31, other arithmetic, combine(): part = part_a * scale_a[..., None] + part_b * scale_b[..., None]  36.3 us
    all_gather x1, blocking collectives, body(): lax.all_gather(w_value, 'req', axis=0, tiled=True)  13.6 us
  transfers between devices with their start and end apart: 4, of which 1 were waited for; matrix products, arithmetic and copies ran while one was open for 7% of the time, Pallas kernels for 0%

commit v1 on v0

v1 whole, which is shorter than its diff:
```python
import functools

import jax
import jax.numpy as jnp
from jax import lax
from jax.experimental import pallas as pl
from jax.experimental.pallas import tpu as pltpu
from jax.sharding import PartitionSpec as P

HEADS = 16
HEAD = 128
SEQ = 32
REQ = 8
ROWS = 32
WIDTH = 2048
SPOTS = 512
MESH = pl.DeviceIdType.MESH
F32 = jnp.float32
BF16 = jnp.bfloat16
NT = (((1,), (1,)), ((), ()))


def layer_norm(values, gain, shift):
    center = values - jnp.mean(values, axis=-1, keepdims=True)
    spread = jnp.mean(center * center, axis=-1, keepdims=True)
    return center * lax.rsqrt(spread + 1e-05) * gain + shift


def far_first(i):
    a, b = i // 4, lax.rem(i, 4)
    dz = 4 + ((a + 1) // 2) * (1 - 2 * lax.rem(a, 2))
    dx = 2 + ((b + 1) // 2) * (1 - 2 * lax.rem(b, 2))
    return dz, dx


def unfold(slots, j):
    first = slots[2 * j].astype(F32)
    second = slots[2 * j + 1].astype(F32)
    low = lax.broadcasted_iota(jnp.int32, (16, 128), 1) < 64
    top = jnp.where(low, first, pltpu.roll(second, 64, 1))
    bottom = jnp.where(low, pltpu.roll(first, 64, 1), second)
    return jnp.concatenate([top, bottom], axis=0)


def kernel(
    lengths,
    tokens,
    cache_keys,
    cache_values,
    gain1,
    bias1,
    wq,
    bq,
    wk,
    bk,
    wv,
    bv,
    wo,
    bo,
    gain2,
    bias2,
    wu,
    bu,
    wd,
    bd,
    out,
    out_keys,
    out_values,
    x_buf,
    n_buf,
    k_buf,
    v_buf,
    wq_g,
    wkvo_g,
    wu_g,
    wd_g,
    q_g,
    kv_g,
    p_s,
    p_g,
    t_s,
    t_g,
    a_g,
    o_g,
    f_s,
    f_g,
    h_g,
    load_sem,
    store_sem,
    send_sem,
    recv_sem,
):
    s = lax.axis_index("seq")
    r = lax.axis_index("req")
    z, x = s // 4, lax.rem(s, 4)
    y, core = r // 2, lax.rem(r, 2)
    sibling = y * 2 + 1 - core
    head, half = s // 2, lax.rem(s, 2)

    barrier = pltpu.get_barrier_semaphore()

    def far(i):
        dz, dx = far_first(i)
        return lax.rem(z + dz, 8) * 4 + lax.rem(x + dx, 4)

    def greet_seq(i, _):
        pl.semaphore_signal(barrier, inc=1, device_id=(far(i), r), device_id_type=MESH)
        return 0

    def greet_req(k, _):
        pl.semaphore_signal(barrier, inc=1, device_id=(s, lax.rem(r + k, REQ)), device_id_type=MESH)
        return 0

    lax.fori_loop(0, SEQ - 1, greet_seq, 0)
    lax.fori_loop(1, REQ, greet_req, 0)

    loads = [
        (wq, wq_g.at[r]),
        (wk, wkvo_g.at[r, 0]),
        (wv, wkvo_g.at[r, 1]),
        (wo, wkvo_g.at[r, 2]),
        (wu, wu_g.at[r]),
        (wd, wd_g.at[r]),
        (cache_keys, k_buf),
        (cache_values, v_buf),
    ]
    loads = [pltpu.make_async_copy(a, b, load_sem.at[i]) for i, (a, b) in enumerate(loads)]
    for load in loads:
        load.start()

    for i in range(8):
        x_buf[4 * i : 4 * i + 4, :] = tokens[i].astype(F32)
    n_buf[...] = layer_norm(x_buf[...], gain1[...], bias1[...]).astype(BF16)

    def send(src, dst, phase, device):
        pltpu.make_async_remote_copy(
            src, dst, send_sem.at[phase], recv_sem.at[phase], device_id=device, device_id_type=MESH
        ).start()

    def received(ref, phase):
        pltpu.make_async_remote_copy(
            ref, ref, send_sem.at[phase], recv_sem.at[phase], device_id=(s, sibling), device_id_type=MESH
        ).wait_recv()

    def sent(ref, phase):
        pltpu.make_async_remote_copy(
            ref, ref, send_sem.at[phase], recv_sem.at[phase], device_id=(s, sibling), device_id_type=MESH
        ).wait_send()

    def spread(src, slots, phase):
        def one(i, _):
            send(src, slots.at[s], phase, (far(i), r))
            return 0

        lax.fori_loop(0, SEQ - 1, one, 0)

    def along_y(buf, phase):
        for k in (2, 1, 3):
            send(buf.at[r], buf.at[r], phase, (s, lax.rem(y + k, 4) * 2 + core))

    def across(buf, phase, own):
        for k in (0,) if own else (1, 3, 2):
            block = lax.rem(y + k, 4) * 2 + core
            send(buf.at[block], buf.at[block], phase, (s, sibling))

    for load in loads[:4]:
        load.wait()
    pl.semaphore_wait(barrier, SEQ - 1 + REQ - 1)

    along_y(wq_g, 0)
    across(wq_g, 1, True)
    along_y(wkvo_g, 2)
    across(wkvo_g, 3, True)
    received(wq_g.at[pl.ds(0, 3)], 0)
    across(wq_g, 1, False)
    received(wq_g.at[pl.ds(0, 4)], 1)

    low = lax.broadcasted_iota(jnp.int32, (16, 128), 1) < 64

    total = jnp.zeros((ROWS, 128), F32)
    for k in range(REQ):
        weight = wq_g[k]
        total += lax.dot_general(
            n_buf[:, 256 * k : 256 * k + 256],
            jnp.concatenate([weight, weight], axis=0),
            NT,
            preferred_element_type=F32,
        )
    total += jnp.concatenate([bq[...], bq[...]], axis=1)
    q_g[s] = jnp.where(low, total[:16], total[16:]).astype(BF16)
    spread(q_g.at[s], q_g, 4)

    received(wkvo_g.at[pl.ds(0, 3)], 2)
    across(wkvo_g, 3, False)
    for load in loads[4:]:
        load.wait()
    received(wkvo_g.at[pl.ds(0, 4)], 3)
    total = jnp.zeros((ROWS, 128), F32)
    for k in range(REQ):
        total += lax.dot_general(
            n_buf[:, 256 * k : 256 * k + 256],
            wkvo_g[k, 0:2].reshape(128, 256),
            NT,
            preferred_element_type=F32,
        )
    total += jnp.concatenate([bk[...], bv[...]], axis=1)
    kv_g[s, 0] = jnp.where(low, total[:16], pltpu.roll(total[16:], 64, 1)).astype(BF16)
    kv_g[s, 1] = jnp.where(low, pltpu.roll(total[:16], 64, 1), total[16:]).astype(BF16)
    spread(kv_g.at[s], kv_g, 5)

    along_y(wu_g, 6)
    across(wu_g, 7, True)
    along_y(wd_g, 8)
    across(wd_g, 9, True)

    scale = HEAD**-0.5
    row = lax.broadcasted_iota(jnp.int32, (ROWS, SPOTS), 0)
    col = lax.broadcasted_iota(jnp.int32, (ROWS, SPOTS), 1)
    limit = jnp.zeros((ROWS, SPOTS), jnp.int32)
    for k in range(8):
        limit = jnp.where((row >> 2) == k, lengths[k], limit)
    valid = ((row >> 2) == (col >> 6)) & ((col & 63) + s * 64 < limit)
    lane = lax.broadcasted_iota(jnp.int32, (ROWS, 128), 1)

    received(q_g.at[pl.ds(0, SEQ - 1)], 4)

    def one_head(j, stats):
        query = unfold(q_g, j).astype(BF16)
        columns = pl.ds(pl.multiple_of(j * 128, 128), 128)
        scores = lax.dot_general(query, k_buf[:, columns], NT, preferred_element_type=F32) * scale
        scores = jnp.where(valid, scores, -1e30)
        peak = jnp.maximum(jnp.max(scores, axis=1, keepdims=True), -1e20)
        expo = jnp.exp(scores - peak)
        amount = jnp.sum(expo, axis=1, keepdims=True)
        part = jnp.dot(expo.astype(BF16), v_buf[:, columns], preferred_element_type=F32)
        p_s[2 * j] = part[:16].astype(BF16)
        p_s[2 * j + 1] = part[16:].astype(BF16)
        return jnp.where(lane == j, peak, jnp.where(lane == j + 16, amount, stats))

    def four_heads(g, stats):
        for j in range(4):
            stats = one_head(4 * g + j, stats)
        return stats

    stats = lax.fori_loop(0, 4, four_heads, jnp.zeros((ROWS, 128), F32))
    turned = stats.T
    turned = jnp.concatenate([turned[:16], turned[16:32], jnp.zeros((16, 64), F32)], axis=1)
    for j in range(HEADS):
        t_s[j] = turned[j : j + 1]

    def share(i, _):
        peer = far(i)
        send(p_s.at[peer], p_g.at[s], 10, (peer, r))
        send(t_s.at[peer // 2], t_g.at[s], 11, (peer, r))
        return 0

    lax.fori_loop(0, SEQ - 1, share, 0)
    p_g[s] = p_s[s]
    t_g[s] = t_s[head]

    received(kv_g.at[pl.ds(0, SEQ - 1)], 5)
    spot = lax.broadcasted_iota(jnp.int32, (SPOTS, ROWS), 0)
    new = lax.broadcasted_iota(jnp.int32, (SPOTS, ROWS), 1)
    start = jnp.zeros((SPOTS, ROWS), jnp.int32)
    for k in range(8):
        start = jnp.where((new >> 2) == k, lengths[k], start)
    hit = ((new >> 2) == (spot >> 6)) & ((spot & 63) + s * 64 == start + (new & 3))
    pick = jnp.where(hit, 1.0, 0.0)
    changed = jnp.max(pick, axis=1, keepdims=True) > 0.5
    pick = pick.astype(BF16)

    def renew(which, buf):
        def one(j, _):
            columns = pl.ds(pl.multiple_of(j * 128, 128), 128)
            rows = unfold(kv_g.at[:, which], j).astype(BF16)
            fresh = jnp.dot(pick, rows, preferred_element_type=F32)
            buf[:, columns] = jnp.where(changed, fresh, buf[:, columns].astype(F32)).astype(BF16)
            return 0

        lax.fori_loop(0, HEADS, one, 0)

    renew(0, k_buf)
    store_keys = pltpu.make_async_copy(k_buf, out_keys, store_sem.at[0])
    store_keys.start()

    def mine(slots):
        return unfold(slots, head)

    query = mine(q_g)
    query = jnp.where(half == 0, query[:16], query[16:]).astype(BF16)
    fresh_keys = mine(kv_g.at[:, 0]).astype(BF16)
    fresh_values = mine(kv_g.at[:, 1]).astype(BF16)
    row = lax.broadcasted_iota(jnp.int32, (16, ROWS), 0) + half * 16
    col = lax.broadcasted_iota(jnp.int32, (16, ROWS), 1)
    scores = lax.dot_general(query, fresh_keys, NT, preferred_element_type=F32) * scale
    scores = jnp.where(((row >> 2) == (col >> 2)) & ((col & 3) <= (row & 3)), scores, -1e30)
    peak_new = jnp.max(scores, axis=1, keepdims=True)
    expo = jnp.exp(scores - peak_new)
    total_new = jnp.sum(expo, axis=1, keepdims=True)
    part_new = jnp.dot(expo.astype(BF16), fresh_values, preferred_element_type=F32)

    received(t_g.at[pl.ds(0, SEQ - 1)], 11)
    turned = t_g[...].reshape(SEQ, 128).T
    peaks = jnp.where(half == 0, turned[0:16], turned[16:32])
    totals = jnp.where(half == 0, turned[32:48], turned[48:64])
    peak = jnp.maximum(jnp.max(peaks, axis=1, keepdims=True), peak_new)
    share_new = jnp.exp(peak_new - peak)
    shares = jnp.exp(peaks - peak)
    total = jnp.sum(shares * totals, axis=1, keepdims=True) + share_new * total_new
    received(p_g.at[pl.ds(0, SEQ - 1)], 10)
    mixed = share_new * part_new
    for k in range(SEQ):
        mixed += shares[:, k : k + 1] * p_g[k].astype(F32)
    a_g[s] = (mixed / total).astype(BF16)
    spread(a_g.at[s], a_g, 12)

    received(wu_g.at[pl.ds(0, 3)], 6)
    across(wu_g, 7, False)
    received(wd_g.at[pl.ds(0, 3)], 8)
    across(wd_g, 9, False)
    renew(1, v_buf)
    store_values = pltpu.make_async_copy(v_buf, out_values, store_sem.at[1])
    store_values.start()

    received(a_g.at[pl.ds(0, SEQ - 1)], 12)
    total = jnp.zeros((ROWS, 128), F32)
    for k in range(REQ):
        left = jnp.concatenate([a_g[4 * k], a_g[4 * k + 1]], axis=0)
        right = jnp.concatenate([a_g[4 * k + 2], a_g[4 * k + 3]], axis=0)
        weight = wkvo_g[k, 2]
        total += lax.dot_general(
            jnp.concatenate([left, right], axis=1),
            jnp.concatenate([weight, weight], axis=0),
            NT,
            preferred_element_type=F32,
        )
    total += jnp.concatenate([bo[...], bo[...]], axis=1)
    o_g[s] = jnp.where(low, total[:16], total[16:]).astype(BF16)
    spread(o_g.at[s], o_g, 13)
    received(wu_g.at[pl.ds(0, 4)], 7)
    received(wd_g.at[pl.ds(0, 4)], 9)
    received(o_g.at[pl.ds(0, SEQ - 1)], 13)

    for j in range(HEADS):
        x_buf[:, 128 * j : 128 * j + 128] += unfold(o_g, j)
    n_buf[...] = layer_norm(x_buf[...], gain2[...], bias2[...]).astype(BF16)
    total = jnp.zeros((ROWS, 256), F32)
    for k in range(REQ):
        total += jnp.dot(n_buf[:, 256 * k : 256 * k + 256], wu_g[k], preferred_element_type=F32)
    total += bu[...]
    hidden = (0.5 * total * (1.0 + lax.erf(total * (0.5**0.5)))).astype(BF16)
    for k in range(REQ):
        feed = jnp.dot(hidden, wd_g[k], preferred_element_type=F32).astype(BF16)
        f_s[4 * k] = feed[:16, :128]
        f_s[4 * k + 1] = feed[16:, :128]
        f_s[4 * k + 2] = feed[:16, 128:]
        f_s[4 * k + 3] = feed[16:, 128:]

    def scatter(i, _):
        peer = far(i)
        send(f_s.at[peer], f_g.at[s], 14, (peer, r))
        return 0

    lax.fori_loop(0, SEQ - 1, scatter, 0)
    f_g[s] = f_s[s]
    columns = pl.ds(pl.multiple_of(head * 128, 128), 128)
    mid = x_buf[pl.ds(pl.multiple_of(half * 16, 16), 16), columns] + bd[:, columns]
    received(f_g.at[pl.ds(0, SEQ - 1)], 14)
    summed = f_g[0].astype(F32)
    for k in range(1, SEQ):
        summed += f_g[k].astype(F32)
    h_g[s] = (mid + summed).astype(BF16)
    spread(h_g.at[s], h_g, 15)

    store_keys.wait()
    store_values.wait()
    for buf, phase in ((wq_g, 0), (wkvo_g, 2), (wu_g, 6), (wd_g, 8)):
        sent(buf.at[pl.ds(0, 3)], phase)
        sent(buf.at[pl.ds(0, 4)], phase + 1)
    for buf, phase in ((q_g, 4), (kv_g, 5), (p_g, 10), (t_g, 11), (a_g, 12), (o_g, 13), (f_g, 14)):
        sent(buf.at[pl.ds(0, SEQ - 1)], phase)
    received(h_g.at[pl.ds(0, SEQ - 1)], 15)
    for j in range(HEADS):
        out[0:16, 128 * j : 128 * j + 128] = h_g[2 * j]
        out[16:32, 128 * j : 128 * j + 128] = h_g[2 * j + 1]
    sent(h_g.at[pl.ds(0, SEQ - 1)], 15)


def body(
    tokens,
    lengths,
    cache_keys,
    cache_values,
    norm1_gain,
    norm1_bias,
    w_query,
    b_query,
    w_key,
    b_key,
    w_value,
    b_value,
    w_out,
    b_out,
    norm2_gain,
    norm2_bias,
    w_up,
    b_up,
    w_down,
    b_down,
):
    vmem = pl.BlockSpec(memory_space=pltpu.VMEM)
    smem = pl.BlockSpec(memory_space=pltpu.SMEM)
    anywhere = pl.BlockSpec(memory_space=pl.ANY)

    def line(v):
        return v.reshape(1, -1)

    slots = pltpu.VMEM((SEQ, 16, 128), BF16)
    hidden_out, new_keys, new_values = pl.pallas_call(
        kernel,
        out_shape=(
            jax.ShapeDtypeStruct((ROWS, WIDTH), BF16),
            jax.ShapeDtypeStruct((SPOTS, WIDTH), BF16),
            jax.ShapeDtypeStruct((SPOTS, WIDTH), BF16),
        ),
        in_specs=[smem, vmem, anywhere, anywhere, vmem, vmem]
        + [anywhere, vmem] * 4
        + [vmem, vmem, anywhere, vmem, anywhere, vmem],
        out_specs=(vmem, anywhere, anywhere),
        scratch_shapes=[
            pltpu.VMEM((ROWS, WIDTH), F32),
            pltpu.VMEM((ROWS, WIDTH), BF16),
            pltpu.VMEM((SPOTS, WIDTH), BF16),
            pltpu.VMEM((SPOTS, WIDTH), BF16),
            pltpu.VMEM((REQ, 64, 256), BF16),
            pltpu.VMEM((REQ, 3, 64, 256), BF16),
            pltpu.VMEM((REQ, 256, 256), BF16),
            pltpu.VMEM((REQ, 256, 256), BF16),
            slots,
            pltpu.VMEM((SEQ, 2, 16, 128), BF16),
            slots,
            slots,
            pltpu.VMEM((HEADS, 1, 128), F32),
            pltpu.VMEM((SEQ, 1, 128), F32),
            slots,
            slots,
            slots,
            slots,
            slots,
            pltpu.SemaphoreType.DMA((8,)),
            pltpu.SemaphoreType.DMA((2,)),
            pltpu.SemaphoreType.DMA((16,)),
            pltpu.SemaphoreType.DMA((16,)),
        ],
        compiler_params=pltpu.CompilerParams(
            collective_id=0, has_side_effects=True, vmem_limit_bytes=40 * 1024 * 1024
        ),
        cost_estimate=pl.CostEstimate(flops=500_000_000, bytes_accessed=9_000_000, transcendentals=300_000),
    )(
        lengths,
        tokens,
        cache_keys.reshape(SPOTS, WIDTH),
        cache_values.reshape(SPOTS, WIDTH),
        line(norm1_gain),
        line(norm1_bias),
        w_query.T,
        line(b_query),
        w_key.T,
        line(b_key),
        w_value.T,
        line(b_value),
        w_out.T,
        line(b_out),
        line(norm2_gain),
        line(norm2_bias),
        w_up,
        line(b_up),
        w_down,
        line(b_down),
    )
    return (
        hidden_out.reshape(8, 4, WIDTH),
        new_keys.reshape(8, 64, WIDTH),
        new_values.reshape(8, 64, WIDTH),
    )


def solution(mesh):
    in_specs = (
        P("req", None, None),
        P("req"),
        P("req", "seq", None),
        P("req", "seq", None),
        P(),
        P(),
        P("req", "seq"),
        P("seq"),
        P("req", "seq"),
        P("seq"),
        P("req", "seq"),
        P("seq"),
        P("req", "seq"),
        P("seq"),
        P(),
        P(),
        P("req", "seq"),
        P("seq"),
        P("seq", "req"),
        P(),
    )
    out_specs = (P("req", None, None), P("req", "seq", None), P("req", "seq", None))
    return jax.shard_map(body, mesh=mesh, in_specs=in_specs, out_specs=out_specs, check_vma=False)
```

time: 583 us -> 85.9 us (0.15)
  blocking collectives: 352 us -> 0 us
  waiting for transfers between devices: 140 us -> 0 us
  Pallas kernels: 0 us -> 61.6 us
  other arithmetic: 47.2 us -> 0 us
  between operations: 14.1 us -> 0.69 us
  matrix products: 7.72 us -> 0 us
    all_gather x10 -> x0, blocking collectives: 352 us -> none  [the longest x2 94.9 us: merged(): lax.all_gather(part.astype(kind), axis)]
    psum x1 -> x0, waiting for transfers between devices: 139 us -> none  [body(): summed = lax.psum(feed.astype(jnp.bfloat16), 'seq').astype(jnp.float32)]
    pallas_call x0 -> x1, Pallas kernels: none -> 61.6 us  [body(): pl.pallas_call(kernel, out_shape=(jax.ShapeDtypeStruct((ROWS, WIDTH), BF1...]
    add x65 -> x0, other arithmetic: 38.9 us -> none  [the longest x31 36.3 us: combine(): part = part_a * scale_a[..., None] + part_b * scale_b[..., None]]
    unnamed x41 -> x44, local copies, waits for them, and re-layouts: 8.23 us -> 22.1 us
    dot_general x8 -> x0, matrix products: 7.72 us -> none  [the longest x1 2.22 us: body(): jnp.dot(hidden, lax.all_gather(w_down, 'req', axis=1, tiled=True), prefer...]
    slice x2 -> x0, local copies, waits for them, and re-layouts: 7.62 us -> none  [the longest x1 3.81 us: body(): new_values = jnp.where(hit, value_rows[:, step][:, None, :], new_values)]
  transfers between devices with their start and end apart: 4 -> 0, of which waited for: 1 -> 0; matrix products, arithmetic and copies ran while one was open for 7% -> 0% of each run, Pallas kernels for 0% -> 0%
where the time goes in v1:
time: 85.9 us; the launch traced here: 85.2 us
  Pallas kernels  61.6 us (72%)
  local copies, waits for them, and re-layouts  22.8 us (27%)
    pallas_call x1, Pallas kernels, body(): pl.pallas_call(kernel, out_shape=(jax.ShapeDtypeStruct((ROWS, WIDTH), BF1...  61.6 us
    unnamed x44, local copies, waits for them, and re-layouts  22.1 us

profile of v1, /device:TPU:2, one launch (start us, length us, event | category | flops | bytes accessed | tf_op | source)
XLA Modules:
  0.0 85.2 jit_solution(17519729760065761639)
XLA Ops:
  0.6 0.0 copy-start
  0.6 1.6 %copy-done = bf16[8,64,2048]{2,1,0:T(8,128)(2,1)S(1)} copy-done((bf16[8,64,2048]{2,1,0:T(8,128)(2,1)S(1)}, bf16[8,64,2048]{2,1,0:T(8,128)(2,1)}, u32[]{:S(2)}) %copy-start) | copy-done | bytes 2097176
  2.2 0.0 copy-start.1
  2.2 1.6 %copy-done.1 = bf16[8,64,2048]{2,1,0:T(8,128)(2,1)S(1)} copy-done((bf16[8,64,2048]{2,1,0:T(8,128)(2,1)S(1)}, bf16[8,64,2048]{2,1,0:T(8,128)(2,1)}, u32[]{:S(2)}) %copy-start.1) | copy-done | bytes 2097176
  3.8 0.0 copy-start.3
  3.8 0.9 %copy-done.3 = bf16[8,4,2048]{2,1,0:T(4,128)(2,1)S(1)} copy-done((bf16[8,4,2048]{2,1,0:T(4,128)(2,1)S(1)}, bf16[8,4,2048]{2,1,0:T(4,128)(2,1)}, u32[]{:S(2)}) %copy-start.3) | copy-done | bytes 131096
  4.7 0.0 copy-start.4
  4.7 0.9 %copy-done.4 = bf16[256,256]{1,0:T(8,128)(2,1)S(1)} copy-done((bf16[256,256]{1,0:T(8,128)(2,1)S(1)}, bf16[256,256]{1,0:T(8,128)(2,1)}, u32[]{:S(2)}) %copy-start.4) | copy-done | bytes 131096
  5.6 0.0 copy-start.5
  5.6 0.9 %copy-done.5 = bf16[256,256]{1,0:T(8,128)(2,1)S(1)} copy-done((bf16[256,256]{1,0:T(8,128)(2,1)S(1)}, bf16[256,256]{1,0:T(8,128)(2,1)}, u32[]{:S(2)}) %copy-start.5) | copy-done | bytes 131096
  6.5 0.0 copy-start.6
  6.5 0.8 copy-done.6
  7.3 0.0 copy-start.7
  7.3 0.8 copy-done.7
  8.1 0.0 copy-start.8
  8.1 0.8 copy-done.8
  8.8 0.0 copy-start.9
  8.8 0.8 copy-done.9
  9.6 0.0 copy-start.10
  9.6 0.7 copy-done.10
  10.3 0.0 copy-start.11
  10.3 0.7 copy-done.11
  11.0 0.0 copy-start.12
  11.0 0.7 copy-done.12
  11.7 0.0 copy-start.13
  11.7 0.7 copy-done.13
  12.4 0.0 copy-start.14
  12.4 0.7 copy-done.14
  13.1 0.0 copy-start.15
  13.1 0.7 copy-done.15
  13.7 0.0 copy-start.16
  13.7 0.7 copy-done.16
  14.4 0.0 copy-start.17
  14.4 0.7 copy-done.17
  15.0 0.0 copy-start.18
  15.1 0.7 copy-done.18
  15.7 0.0 copy-start.19
  15.7 0.7 copy-done.19
  16.4 0.0 copy-start.20
  16.4 0.7 copy-done.20
  17.0 61.6 %shard_map.211 = (bf16[32,2048]{1,0:T(8,128)(2,1)S(1)}, bf16[512,2048]{1,0:T(8,128)(2,1)S(1)}, bf16[512,2048]{1,0:T(8,128)(2,1)S(1)}) custom-call(s32[8]{0:T(128)S(1)} %copy-done.16, bf16[8,4,2048]{2,1,0:T(4,128)(2,1)S(1)} %copy-done.3, bf16[512,2048]{1,0:T(8,128)(2,1)S(1)} %bitcast.18, bf16[512,2048]{1,0:T(8,128)(2,1)S(1)} %bitcast.19, ...), custom_call_target="tpu_custom_call" | custom-call | flops 500000000 | bytes 9000000 | tf_op jit(solution)/shard_map/pallas_call | solution.py:419
  78.7 0.0 copy-start.2
  78.7 1.3 %copy-done.2 = bf16[512,2048]{1,0:T(8,128)(2,1)} copy-done((bf16[512,2048]{1,0:T(8,128)(2,1)}, bf16[512,2048]{1,0:T(8,128)(2,1)S(1)}, u32[]{:S(2)}) %copy-start.2) | copy-done | bytes 2097176
  80.0 0.7 reshape.63
  80.7 3.2 %copy.25 = bf16[8,64,2048]{2,1,0:T(8,128)(2,1)} copy(bf16[8,64,2048]{2,1,0:T(8,128)(2,1)} %bitcast.21) | data formatting | bytes 4194304
  83.9 1.3 %copy.26 = bf16[8,64,2048]{2,1,0:T(8,128)(2,1)} copy(bf16[8,64,2048]{2,1,0:T(8,128)(2,1)S(1)} %bitcast.20) | data formatting | bytes 4194304
Async XLA Ops:
  0.6 1.6 %copy-start = (bf16[8,64,2048]{2,1,0:T(8,128)(2,1)S(1)}, bf16[8,64,2048]{2,1,0:T(8,128)(2,1)}, u32[]{:S(2)}) copy-start(bf16[8,64,2048]{2,1,0:T(8,128)(2,1)} %param.22) | copy-start | bytes 6291460
  2.2 1.6 %copy-start.1 = (bf16[8,64,2048]{2,1,0:T(8,128)(2,1)S(1)}, bf16[8,64,2048]{2,1,0:T(8,128)(2,1)}, u32[]{:S(2)}) copy-start(bf16[8,64,2048]{2,1,0:T(8,128)(2,1)} %param.23) | copy-start | bytes 6291460
  3.8 0.9 %copy-start.3 = (bf16[8,4,2048]{2,1,0:T(4,128)(2,1)S(1)}, bf16[8,4,2048]{2,1,0:T(4,128)(2,1)}, u32[]{:S(2)}) copy-start(bf16[8,4,2048]{2,1,0:T(4,128)(2,1)} %tokens.1) | copy-start | bytes 393220
  4.7 0.9 %copy-start.4 = (bf16[256,256]{1,0:T(8,128)(2,1)S(1)}, bf16[256,256]{1,0:T(8,128)(2,1)}, u32[]{:S(2)}) copy-start(bf16[256,256]{1,0:T(8,128)(2,1)} %wu.1) | copy-start | bytes 393220
  5.6 0.9 %copy-start.5 = (bf16[256,256]{1,0:T(8,128)(2,1)S(1)}, bf16[256,256]{1,0:T(8,128)(2,1)}, u32[]{:S(2)}) copy-start(bf16[256,256]{1,0:T(8,128)(2,1)} %wd.1) | copy-start | bytes 393220
  6.5 0.8 copy-start.6
  7.3 0.8 copy-start.7
  8.1 0.8 copy-start.8
  8.8 0.8 copy-start.9
  9.6 0.7 copy-start.10
  10.3 0.7 copy-start.11
  11.0 0.7 copy-start.12
  11.7 0.7 copy-start.13
  12.4 0.7 copy-start.14
  13.1 0.7 copy-start.15
  13.7 0.7 copy-start.16
  14.4 0.7 copy-start.17
  15.0 0.7 copy-start.18
  15.7 0.7 copy-start.19
  16.4 0.7 copy-start.20
  78.7 1.3 %copy-start.2 = (bf16[512,2048]{1,0:T(8,128)(2,1)}, bf16[512,2048]{1,0:T(8,128)(2,1)S(1)}, u32[]{:S(2)}) copy-start(bf16[512,2048]{1,0:T(8,128)(2,1)S(1)} %get-tuple-element.7) | copy-start | bytes 6291460

commit v2 on v1

--- a/solution.py
+++ b/solution.py
@@ -70,6 +70,18 @@
     n_buf,
     k_buf,
     v_buf,
+    lengths_s,
+    tokens_s,
+    gain1_s,
+    bias1_s,
+    bq_s,
+    bk_s,
+    bv_s,
+    bo_s,
+    gain2_s,
+    bias2_s,
+    bu_s,
+    bd_s,
     wq_g,
     wkvo_g,
     wu_g,
@@ -115,12 +127,24 @@
     lax.fori_loop(1, REQ, greet_req, 0)
 
     loads = [
+        (tokens, tokens_s),
+        (gain1, gain1_s),
+        (bias1, bias1_s),
         (wq, wq_g.at[r]),
         (wk, wkvo_g.at[r, 0]),
         (wv, wkvo_g.at[r, 1]),
         (wo, wkvo_g.at[r, 2]),
+        (bq, bq_s),
+        (bk, bk_s),
+        (bv, bv_s),
+        (bo, bo_s),
+        (lengths, lengths_s),
         (wu, wu_g.at[r]),
         (wd, wd_g.at[r]),
+        (gain2, gain2_s),
+        (bias2, bias2_s),
+        (bu, bu_s),
+        (bd, bd_s),
         (cache_keys, k_buf),
         (cache_values, v_buf),
     ]
@@ -128,9 +152,11 @@
     for load in loads:
         load.start()
 
+    for load in loads[:3]:
+        load.wait()
     for i in range(8):
-        x_buf[4 * i : 4 * i + 4, :] = tokens[i].astype(F32)
-    n_buf[...] = layer_norm(x_buf[...], gain1[...], bias1[...]).astype(BF16)
+        x_buf[4 * i : 4 * i + 4, :] = tokens_s[i].astype(F32)
+    n_buf[...] = layer_norm(x_buf[...], gain1_s[...], bias1_s[...]).astype(BF16)
 
     def send(src, dst, phase, device):
         pltpu.make_async_remote_copy(
@@ -163,7 +189,7 @@
             block = lax.rem(y + k, 4) * 2 + core
             send(buf.at[block], buf.at[block], phase, (s, sibling))
 
-    for load in loads[:4]:
+    for load in loads[3:12]:
         load.wait()
     pl.semaphore_wait(barrier, SEQ - 1 + REQ - 1)
 
@@ -186,13 +212,13 @@
             NT,
             preferred_element_type=F32,
         )
-    total += jnp.concatenate([bq[...], bq[...]], axis=1)
+    total += jnp.concatenate([bq_s[...], bq_s[...]], axis=1)
     q_g[s] = jnp.where(low, total[:16], total[16:]).astype(BF16)
     spread(q_g.at[s], q_g, 4)
 
     received(wkvo_g.at[pl.ds(0, 3)], 2)
     across(wkvo_g, 3, False)
-    for load in loads[4:]:
+    for load in loads[12:]:
         load.wait()
     received(wkvo_g.at[pl.ds(0, 4)], 3)
     total = jnp.zeros((ROWS, 128), F32)
@@ -203,7 +229,7 @@
             NT,
             preferred_element_type=F32,
         )
-    total += jnp.concatenate([bk[...], bv[...]], axis=1)
+    total += jnp.concatenate([bk_s[...], bv_s[...]], axis=1)
     kv_g[s, 0] = jnp.where(low, total[:16], pltpu.roll(total[16:], 64, 1)).astype(BF16)
     kv_g[s, 1] = jnp.where(low, pltpu.roll(total[:16], 64, 1), total[16:]).astype(BF16)
     spread(kv_g.at[s], kv_g, 5)
@@ -218,7 +244,7 @@
     col = lax.broadcasted_iota(jnp.int32, (ROWS, SPOTS), 1)
     limit = jnp.zeros((ROWS, SPOTS), jnp.int32)
     for k in range(8):
-        limit = jnp.where((row >> 2) == k, lengths[k], limit)
+        limit = jnp.where((row >> 2) == k, lengths_s[k], limit)
     valid = ((row >> 2) == (col >> 6)) & ((col & 63) + s * 64 < limit)
     lane = lax.broadcasted_iota(jnp.int32, (ROWS, 128), 1)
 
@@ -263,7 +289,7 @@
     new = lax.broadcasted_iota(jnp.int32, (SPOTS, ROWS), 1)
     start = jnp.zeros((SPOTS, ROWS), jnp.int32)
     for k in range(8):
-        start = jnp.where((new >> 2) == k, lengths[k], start)
+        start = jnp.where((new >> 2) == k, lengths_s[k], start)
     hit = ((new >> 2) == (spot >> 6)) & ((spot & 63) + s * 64 == start + (new & 3))
     pick = jnp.where(hit, 1.0, 0.0)
     changed = jnp.max(pick, axis=1, keepdims=True) > 0.5
@@ -334,7 +360,7 @@
             NT,
             preferred_element_type=F32,
         )
-    total += jnp.concatenate([bo[...], bo[...]], axis=1)
+    total += jnp.concatenate([bo_s[...], bo_s[...]], axis=1)
     o_g[s] = jnp.where(low, total[:16], total[16:]).astype(BF16)
     spread(o_g.at[s], o_g, 13)
     received(wu_g.at[pl.ds(0, 4)], 7)
@@ -343,11 +369,11 @@
 
     for j in range(HEADS):
         x_buf[:, 128 * j : 128 * j + 128] += unfold(o_g, j)
-    n_buf[...] = layer_norm(x_buf[...], gain2[...], bias2[...]).astype(BF16)
+    n_buf[...] = layer_norm(x_buf[...], gain2_s[...], bias2_s[...]).astype(BF16)
     total = jnp.zeros((ROWS, 256), F32)
     for k in range(REQ):
         total += jnp.dot(n_buf[:, 256 * k : 256 * k + 256], wu_g[k], preferred_element_type=F32)
-    total += bu[...]
+    total += bu_s[...]
     hidden = (0.5 * total * (1.0 + lax.erf(total * (0.5**0.5)))).astype(BF16)
     for k in range(REQ):
         feed = jnp.dot(hidden, wd_g[k], preferred_element_type=F32).astype(BF16)
@@ -364,7 +390,7 @@
     lax.fori_loop(0, SEQ - 1, scatter, 0)
     f_g[s] = f_s[s]
     columns = pl.ds(pl.multiple_of(head * 128, 128), 128)
-    mid = x_buf[pl.ds(pl.multiple_of(half * 16, 16), 16), columns] + bd[:, columns]
+    mid = x_buf[pl.ds(pl.multiple_of(half * 16, 16), 16), columns] + bd_s[:, columns]
     received(f_g.at[pl.ds(0, SEQ - 1)], 14)
     summed = f_g[0].astype(F32)
     for k in range(1, SEQ):
@@ -381,9 +407,28 @@
         sent(buf.at[pl.ds(0, SEQ - 1)], phase)
     received(h_g.at[pl.ds(0, SEQ - 1)], 15)
     for j in range(HEADS):
-        out[0:16, 128 * j : 128 * j + 128] = h_g[2 * j]
-        out[16:32, 128 * j : 128 * j + 128] = h_g[2 * j + 1]
+        whole = jnp.concatenate([h_g[2 * j], h_g[2 * j + 1]], axis=0).astype(F32)
+        for i in range(8):
+            out[i, :, 128 * j : 128 * j + 128] = whole[4 * i : 4 * i + 4].astype(BF16)
     sent(h_g.at[pl.ds(0, SEQ - 1)], 15)
+
+
+def finish(hidden, keys, values, out, out_keys, out_values, h_buf, k_buf, v_buf, in_sem, out_sem):
+    half = SPOTS // 2
+    moves = [(hidden, h_buf, out)]
+    for a, b, c in ((keys, k_buf, out_keys), (values, v_buf, out_values)):
+        for i in range(2):
+            part = pl.ds(i * half, half)
+            moves.append((a.at[part], b.at[part], c.at[part]))
+    ins = [pltpu.make_async_copy(a, b, in_sem.at[i]) for i, (a, b, _) in enumerate(moves)]
+    outs = [pltpu.make_async_copy(b, c, out_sem.at[i]) for i, (_, b, c) in enumerate(moves)]
+    for copy in ins:
+        copy.start()
+    for arrived, copy in zip(ins, outs):
+        arrived.wait()
+        copy.start()
+    for copy in outs:
+        copy.wait()
 
 
 def body(
@@ -409,8 +454,7 @@
     b_down,
 ):
     vmem = pl.BlockSpec(memory_space=pltpu.VMEM)
-    smem = pl.BlockSpec(memory_space=pltpu.SMEM)
-    anywhere = pl.BlockSpec(memory_space=pl.ANY)
+    hbm = pl.BlockSpec(memory_space=pltpu.HBM)
 
     def line(v):
         return v.reshape(1, -1)
@@ -419,19 +463,29 @@
     hidden_out, new_keys, new_values = pl.pallas_call(
         kernel,
         out_shape=(
-            jax.ShapeDtypeStruct((ROWS, WIDTH), BF16),
+            jax.ShapeDtypeStruct((8, 4, WIDTH), BF16),
             jax.ShapeDtypeStruct((SPOTS, WIDTH), BF16),
             jax.ShapeDtypeStruct((SPOTS, WIDTH), BF16),
         ),
-        in_specs=[smem, vmem, anywhere, anywhere, vmem, vmem]
-        + [anywhere, vmem] * 4
-        + [vmem, vmem, anywhere, vmem, anywhere, vmem],
-        out_specs=(vmem, anywhere, anywhere),
+        in_specs=[hbm] * 20,
+        out_specs=(vmem, hbm, hbm),
         scratch_shapes=[
             pltpu.VMEM((ROWS, WIDTH), F32),
             pltpu.VMEM((ROWS, WIDTH), BF16),
             pltpu.VMEM((SPOTS, WIDTH), BF16),
             pltpu.VMEM((SPOTS, WIDTH), BF16),
+            pltpu.SMEM((8,), jnp.int32),
+            pltpu.VMEM((8, 4, WIDTH), BF16),
+            pltpu.VMEM((1, WIDTH), F32),
+            pltpu.VMEM((1, WIDTH), F32),
+            pltpu.VMEM((1, 64), F32),
+            pltpu.VMEM((1, 64), F32),
+            pltpu.VMEM((1, 64), F32),
+            pltpu.VMEM((1, 64), F32),
+            pltpu.VMEM((1, WIDTH), F32),
+            pltpu.VMEM((1, WIDTH), F32),
+            pltpu.VMEM((1, 256), F32),
+            pltpu.VMEM((1, WIDTH), F32),
             pltpu.VMEM((REQ, 64, 256), BF16),
             pltpu.VMEM((REQ, 3, 64, 256), BF16),
             pltpu.VMEM((REQ, 256, 256), BF16),
@@ -447,13 +501,13 @@
             slots,
             slots,
             slots,
-            pltpu.SemaphoreType.DMA((8,)),
+            pltpu.SemaphoreType.DMA((20,)),
             pltpu.SemaphoreType.DMA((2,)),
             pltpu.SemaphoreType.DMA((16,)),
             pltpu.SemaphoreType.DMA((16,)),
         ],
         compiler_params=pltpu.CompilerParams(
-            collective_id=0, has_side_effects=True, vmem_limit_bytes=40 * 1024 * 1024
+            collective_id=0, has_side_effects=True, vmem_limit_bytes=58 * 1024 * 1024
         ),
         cost_estimate=pl.CostEstimate(flops=500_000_000, bytes_accessed=9_000_000, transcendentals=300_000),
     )(
@@ -478,11 +532,25 @@
         w_down,
         line(b_down),
     )
-    return (
-        hidden_out.reshape(8, 4, WIDTH),
-        new_keys.reshape(8, 64, WIDTH),
-        new_values.reshape(8, 64, WIDTH),
-    )
+    hidden_out, new_keys, new_values = pl.pallas_call(
+        finish,
+        out_shape=(
+            jax.ShapeDtypeStruct((8, 4, WIDTH), BF16),
+            jax.ShapeDtypeStruct((SPOTS, WIDTH), BF16),
+            jax.ShapeDtypeStruct((SPOTS, WIDTH), BF16),
+        ),
+        in_specs=[hbm] * 3,
+        out_specs=(hbm, hbm, hbm),
+        scratch_shapes=[
+            pltpu.VMEM((8, 4, WIDTH), BF16),
+            pltpu.VMEM((SPOTS, WIDTH), BF16),
+            pltpu.VMEM((SPOTS, WIDTH), BF16),
+            pltpu.SemaphoreType.DMA((5,)),
+            pltpu.SemaphoreType.DMA((5,)),
+        ],
+        compiler_params=pltpu.CompilerParams(vmem_limit_bytes=58 * 1024 * 1024),
+    )(hidden_out, new_keys, new_values)
+    return hidden_out, new_keys.reshape(8, 64, WIDTH), new_values.reshape(8, 64, WIDTH)
 
 
 def solution(mesh):

time: 85.9 us -> 66 us (0.77)
  local copies, waits for them, and re-layouts: 22.8 us -> 0 us
  Pallas kernels: 61.6 us -> 65.3 us
    unnamed x44 -> x0, local copies, waits for them, and re-layouts: 22.1 us -> none
    pallas_call x1 -> x2, Pallas kernels: 61.6 us -> 65.3 us  [the longest x1 61.8 us: body(): pl.pallas_call(kernel, out_shape=(jax.ShapeDtypeStruct((8, 4, WIDTH), BF1...]
where the time goes in v2:
time: 66 us; the launch traced here: 65.9 us
  Pallas kernels  65.3 us (99%)
    pallas_call x1, Pallas kernels, body(): pl.pallas_call(kernel, out_shape=(jax.ShapeDtypeStruct((8, 4, WIDTH), BF1...  61.8 us
    pallas_call x1, Pallas kernels, body(): pl.pallas_call(finish, out_shape=(jax.ShapeDtypeStruct((8, 4, WIDTH), BF1...  3.5 us

profile of v2, /device:TPU:2, one launch (start us, length us, event | category | flops | bytes accessed | tf_op | source)
XLA Modules:
  0.0 65.9 jit_solution(17610055532451937373)
XLA Ops:
  0.6 61.8 %shard_map.211 = (bf16[8,4,2048]{2,1,0:T(4,128)(2,1)}, bf16[512,2048]{1,0:T(8,128)(2,1)}, bf16[512,2048]{1,0:T(8,128)(2,1)}) custom-call(s32[8]{0:T(128)} %lengths.1, bf16[8,4,2048]{2,1,0:T(4,128)(2,1)} %tokens.1, bf16[512,2048]{1,0:T(8,128)(2,1)} %bitcast.18, bf16[512,2048]{1,0:T(8,128)(2,1)} %bitcast.19, f32[1,2048]{1,0:T(1,128)} %bitcast.24, ...), custom_call_target="tpu_custom_call" | custom-call | flops 500000000 | bytes 9000000 | tf_op jit(solution)/shard_map/pallas_call | solution.py:463
  62.4 3.5 %shard_map.212 = (bf16[8,4,2048]{2,1,0:T(4,128)(2,1)}, bf16[512,2048]{1,0:T(8,128)(2,1)}, bf16[512,2048]{1,0:T(8,128)(2,1)}) custom-call(bf16[8,4,2048]{2,1,0:T(4,128)(2,1)} %get-tuple-element.9.hidden, bf16[512,2048]{1,0:T(8,128)(2,1)} %get-tuple-element.10.keys, bf16[512,2048]{1,0:T(8,128)(2,1)} %get-tuple-element.11.values), custom_call_target="tpu_custom_call" | custom-call | tf_op jit(solution)/shard_map/pallas_call | solution.py:535

commit v3 on v2

--- a/solution.py
+++ b/solution.py
@@ -18,6 +18,12 @@
 F32 = jnp.float32
 BF16 = jnp.bfloat16
 NT = (((1,), (1,)), ((), ()))
+ORDER = (
+    ((0, 0), (0, 1), (1, 0), (7, 0)),
+    ((1, 1), (7, 1), (2, 0), (6, 0)),
+    ((4, 1), (4, 0), (3, 1), (5, 1)),
+    ((3, 0), (5, 0), (2, 1), (6, 1)),
+)
 
 
 def layer_norm(values, gain, shift):
@@ -90,8 +96,6 @@
     kv_g,
     p_s,
     p_g,
-    t_s,
-    t_g,
     a_g,
     o_g,
     f_s,
@@ -101,6 +105,9 @@
     store_sem,
     send_sem,
     recv_sem,
+    query_sem,
+    column_sem,
+    plane_sem,
 ):
     s = lax.axis_index("seq")
     r = lax.axis_index("req")
@@ -108,6 +115,7 @@
     y, core = r // 2, lax.rem(r, 2)
     sibling = y * 2 + 1 - core
     head, half = s // 2, lax.rem(s, 2)
+    partner = s + 1 - 2 * half
 
     barrier = pltpu.get_barrier_semaphore()
 
@@ -115,16 +123,14 @@
         dz, dx = far_first(i)
         return lax.rem(z + dz, 8) * 4 + lax.rem(x + dx, 4)
 
-    def greet_seq(i, _):
-        pl.semaphore_signal(barrier, inc=1, device_id=(far(i), r), device_id_type=MESH)
-        return 0
-
-    def greet_req(k, _):
-        pl.semaphore_signal(barrier, inc=1, device_id=(s, lax.rem(r + k, REQ)), device_id_type=MESH)
-        return 0
-
-    lax.fori_loop(0, SEQ - 1, greet_seq, 0)
-    lax.fori_loop(1, REQ, greet_req, 0)
+    def along(dz, dx):
+        return (lax.rem(z + dz, 8) * 4 + lax.rem(x + dx, 4), r)
+
+    for dz, dx in ((2, 0), (6, 0), (0, 2), (1, 0), (7, 0), (0, 1), (0, 3)):
+        pl.semaphore_signal(barrier, inc=1, device_id=along(dz, dx), device_id_type=MESH)
+    for k in (4, 5, 2, 3, 6, 7, 1):
+        near = lax.rem(y + k // 2, 4) * 2 + lax.rem(core + k, 2)
+        pl.semaphore_signal(barrier, inc=1, device_id=(s, near), device_id_type=MESH)
 
     loads = [
         (tokens, tokens_s),
@@ -191,12 +197,17 @@
 
     for load in loads[3:12]:
         load.wait()
-    pl.semaphore_wait(barrier, SEQ - 1 + REQ - 1)
+    pl.semaphore_wait(barrier, 14)
+    for dz in (2, 6):
+        pl.semaphore_signal(column_sem, inc=1, device_id=along(dz, 0), device_id_type=MESH)
 
     along_y(wq_g, 0)
     across(wq_g, 1, True)
     along_y(wkvo_g, 2)
     across(wkvo_g, 3, True)
+    pl.semaphore_wait(column_sem, 2)
+    for dx in (2, 1, 3):
+        pl.semaphore_signal(plane_sem, inc=1, device_id=along(0, dx), device_id_type=MESH)
     received(wq_g.at[pl.ds(0, 3)], 0)
     across(wq_g, 1, False)
     received(wq_g.at[pl.ds(0, 4)], 1)
@@ -214,12 +225,74 @@
         )
     total += jnp.concatenate([bq_s[...], bq_s[...]], axis=1)
     q_g[s] = jnp.where(low, total[:16], total[16:]).astype(BF16)
-    spread(q_g.at[s], q_g, 4)
+
+    pl.semaphore_wait(plane_sem, 3)
+
+    def share_queries(i, _):
+        pltpu.make_async_remote_copy(
+            q_g.at[s],
+            q_g.at[s],
+            send_sem.at[4],
+            query_sem.at[s],
+            device_id=(far(i), r),
+            device_id_type=MESH,
+        ).start()
+        return 0
+
+    lax.fori_loop(0, SEQ - 1, share_queries, 0)
 
     received(wkvo_g.at[pl.ds(0, 3)], 2)
     across(wkvo_g, 3, False)
     for load in loads[12:]:
         load.wait()
+
+    scale = HEAD**-0.5
+    row = lax.broadcasted_iota(jnp.int32, (ROWS, SPOTS), 0)
+    col = lax.broadcasted_iota(jnp.int32, (ROWS, SPOTS), 1)
+    limit = jnp.zeros((ROWS, SPOTS), jnp.int32)
+    for k in range(8):
+        limit = jnp.where((row >> 2) == k, lengths_s[k], limit)
+    valid = ((row >> 2) == (col >> 6)) & ((col & 63) + s * 64 < limit)
+    lane = lax.broadcasted_iota(jnp.int32, (ROWS, 128), 1)
+    marks = [lane == s + 32 * k for k in range(4)]
+
+    def halves(value):
+        first = value.astype(BF16).astype(F32)
+        return first, (value - first).astype(BF16).astype(F32)
+
+    for group in ORDER:
+        heads = [(lax.rem(z + dz, 8) * 2 + lax.rem(x // 2 + dp, 2), dz + dp == 0) for dz, dp in group]
+        for j, own in heads:
+            for peer in (partner,) if own else (2 * j, 2 * j + 1):
+                pltpu.make_async_copy(q_g.at[peer], q_g.at[peer], query_sem.at[peer]).wait()
+        columns = [pl.ds(pl.multiple_of(j * 128, 128), 128) for j, _ in heads]
+        scores = [
+            lax.dot_general(
+                unfold(q_g, j).astype(BF16), k_buf[:, columns[k]], NT, preferred_element_type=F32
+            )
+            for k, (j, _) in enumerate(heads)
+        ]
+        scores = [jnp.where(valid, score * scale, -1e30) for score in scores]
+        peaks = [halves(jnp.maximum(jnp.max(score, axis=1, keepdims=True), -1e20)) for score in scores]
+        expos = [jnp.exp(score - (peak[0] + peak[1])) for score, peak in zip(scores, peaks)]
+        amounts = [halves(jnp.sum(expo, axis=1, keepdims=True)) for expo in expos]
+        parts = [
+            jnp.dot(expo.astype(BF16), v_buf[:, column], preferred_element_type=F32).astype(BF16)
+            for expo, column in zip(expos, columns)
+        ]
+        for k, (j, own) in enumerate(heads):
+            stats = jnp.zeros((ROWS, 128), F32)
+            for mark, value in zip(marks, peaks[k] + amounts[k]):
+                stats = jnp.where(mark, value, stats)
+            stats = stats.astype(BF16)
+            p_s[2 * j, 0:16] = parts[k][:16]
+            p_s[2 * j, 16:32] = stats[:16]
+            p_s[2 * j + 1, 0:16] = parts[k][16:]
+            p_s[2 * j + 1, 16:32] = stats[16:]
+            for peer in (partner,) if own else (2 * j, 2 * j + 1):
+                send(p_s.at[peer], p_g.at[s], 10, (peer, r))
+    p_g[s] = p_s[s]
+
     received(wkvo_g.at[pl.ds(0, 4)], 3)
     total = jnp.zeros((ROWS, 128), F32)
     for k in range(REQ):
@@ -232,86 +305,28 @@
     total += jnp.concatenate([bk_s[...], bv_s[...]], axis=1)
     kv_g[s, 0] = jnp.where(low, total[:16], pltpu.roll(total[16:], 64, 1)).astype(BF16)
     kv_g[s, 1] = jnp.where(low, pltpu.roll(total[:16], 64, 1), total[16:]).astype(BF16)
-    spread(kv_g.at[s], kv_g, 5)
+    send(kv_g.at[s], kv_g.at[s], 11, (partner, r))
+
+    def share_rows(i, _):
+        peer = far(i)
+
+        @pl.when(peer != partner)
+        def _():
+            send(kv_g.at[s], kv_g.at[s], 5, (peer, r))
+
+        return 0
+
+    lax.fori_loop(0, SEQ - 1, share_rows, 0)
 
     along_y(wu_g, 6)
     across(wu_g, 7, True)
     along_y(wd_g, 8)
     across(wd_g, 9, True)
 
-    scale = HEAD**-0.5
-    row = lax.broadcasted_iota(jnp.int32, (ROWS, SPOTS), 0)
-    col = lax.broadcasted_iota(jnp.int32, (ROWS, SPOTS), 1)
-    limit = jnp.zeros((ROWS, SPOTS), jnp.int32)
-    for k in range(8):
-        limit = jnp.where((row >> 2) == k, lengths_s[k], limit)
-    valid = ((row >> 2) == (col >> 6)) & ((col & 63) + s * 64 < limit)
-    lane = lax.broadcasted_iota(jnp.int32, (ROWS, 128), 1)
-
-    received(q_g.at[pl.ds(0, SEQ - 1)], 4)
-
-    def one_head(j, stats):
-        query = unfold(q_g, j).astype(BF16)
-        columns = pl.ds(pl.multiple_of(j * 128, 128), 128)
-        scores = lax.dot_general(query, k_buf[:, columns], NT, preferred_element_type=F32) * scale
-        scores = jnp.where(valid, scores, -1e30)
-        peak = jnp.maximum(jnp.max(scores, axis=1, keepdims=True), -1e20)
-        expo = jnp.exp(scores - peak)
-        amount = jnp.sum(expo, axis=1, keepdims=True)
-        part = jnp.dot(expo.astype(BF16), v_buf[:, columns], preferred_element_type=F32)
-        p_s[2 * j] = part[:16].astype(BF16)
-        p_s[2 * j + 1] = part[16:].astype(BF16)
-        return jnp.where(lane == j, peak, jnp.where(lane == j + 16, amount, stats))
-
-    def four_heads(g, stats):
-        for j in range(4):
-            stats = one_head(4 * g + j, stats)
-        return stats
-
-    stats = lax.fori_loop(0, 4, four_heads, jnp.zeros((ROWS, 128), F32))
-    turned = stats.T
-    turned = jnp.concatenate([turned[:16], turned[16:32], jnp.zeros((16, 64), F32)], axis=1)
-    for j in range(HEADS):
-        t_s[j] = turned[j : j + 1]
-
-    def share(i, _):
-        peer = far(i)
-        send(p_s.at[peer], p_g.at[s], 10, (peer, r))
-        send(t_s.at[peer // 2], t_g.at[s], 11, (peer, r))
-        return 0
-
-    lax.fori_loop(0, SEQ - 1, share, 0)
-    p_g[s] = p_s[s]
-    t_g[s] = t_s[head]
-
-    received(kv_g.at[pl.ds(0, SEQ - 1)], 5)
-    spot = lax.broadcasted_iota(jnp.int32, (SPOTS, ROWS), 0)
-    new = lax.broadcasted_iota(jnp.int32, (SPOTS, ROWS), 1)
-    start = jnp.zeros((SPOTS, ROWS), jnp.int32)
-    for k in range(8):
-        start = jnp.where((new >> 2) == k, lengths_s[k], start)
-    hit = ((new >> 2) == (spot >> 6)) & ((spot & 63) + s * 64 == start + (new & 3))
-    pick = jnp.where(hit, 1.0, 0.0)
-    changed = jnp.max(pick, axis=1, keepdims=True) > 0.5
-    pick = pick.astype(BF16)
-
-    def renew(which, buf):
-        def one(j, _):
-            columns = pl.ds(pl.multiple_of(j * 128, 128), 128)
-            rows = unfold(kv_g.at[:, which], j).astype(BF16)
-            fresh = jnp.dot(pick, rows, preferred_element_type=F32)
-            buf[:, columns] = jnp.where(changed, fresh, buf[:, columns].astype(F32)).astype(BF16)
-            return 0
-
-        lax.fori_loop(0, HEADS, one, 0)
-
-    renew(0, k_buf)
-    store_keys = pltpu.make_async_copy(k_buf, out_keys, store_sem.at[0])
-    store_keys.start()
-
     def mine(slots):
         return unfold(slots, head)
 
+    received(kv_g.at[0], 11)
     query = mine(q_g)
     query = jnp.where(half == 0, query[:16], query[16:]).astype(BF16)
     fresh_keys = mine(kv_g.at[:, 0]).astype(BF16)
@@ -325,29 +340,55 @@
     total_new = jnp.sum(expo, axis=1, keepdims=True)
     part_new = jnp.dot(expo.astype(BF16), fresh_values, preferred_element_type=F32)
 
-    received(t_g.at[pl.ds(0, SEQ - 1)], 11)
-    turned = t_g[...].reshape(SEQ, 128).T
-    peaks = jnp.where(half == 0, turned[0:16], turned[16:32])
-    totals = jnp.where(half == 0, turned[32:48], turned[48:64])
+    received(p_g.at[pl.ds(0, SEQ - 1)], 10)
+    stats = p_g[0, 16:32].astype(F32)
+    for k in range(1, SEQ):
+        stats += p_g[k, 16:32].astype(F32)
+    stats += pltpu.roll(stats, 96, 1)
+    lane = lax.broadcasted_iota(jnp.int32, (16, 128), 1)
+    peaks = jnp.where(lane < 32, stats, -1e20)
+    totals = jnp.where(lane < 32, pltpu.roll(stats, 64, 1), 0.0)
     peak = jnp.maximum(jnp.max(peaks, axis=1, keepdims=True), peak_new)
     share_new = jnp.exp(peak_new - peak)
     shares = jnp.exp(peaks - peak)
     total = jnp.sum(shares * totals, axis=1, keepdims=True) + share_new * total_new
-    received(p_g.at[pl.ds(0, SEQ - 1)], 10)
     mixed = share_new * part_new
     for k in range(SEQ):
-        mixed += shares[:, k : k + 1] * p_g[k].astype(F32)
+        mixed += shares[:, k : k + 1] * p_g[k, 0:16].astype(F32)
     a_g[s] = (mixed / total).astype(BF16)
     spread(a_g.at[s], a_g, 12)
+
+    received(kv_g.at[pl.ds(0, SEQ - 2)], 5)
+    spot = lax.broadcasted_iota(jnp.int32, (SPOTS, ROWS), 0)
+    new = lax.broadcasted_iota(jnp.int32, (SPOTS, ROWS), 1)
+    start = jnp.zeros((SPOTS, ROWS), jnp.int32)
+    for k in range(8):
+        start = jnp.where((new >> 2) == k, lengths_s[k], start)
+    hit = ((new >> 2) == (spot >> 6)) & ((spot & 63) + s * 64 == start + (new & 3))
+    pick = jnp.where(hit, 1.0, 0.0)
+    changed = jnp.max(pick, axis=1, keepdims=True) > 0.5
+    pick = pick.astype(BF16)
+
+    def renew(which, buf):
+        def four(g, _):
+            columns = [pl.ds(pl.multiple_of((4 * g + j) * 128, 128), 128) for j in range(4)]
+            rows = [unfold(kv_g.at[:, which], 4 * g + j).astype(BF16) for j in range(4)]
+            fresh = [jnp.dot(pick, row, preferred_element_type=F32) for row in rows]
+            for j in range(4):
+                old = buf[:, columns[j]].astype(F32)
+                buf[:, columns[j]] = jnp.where(changed, fresh[j], old).astype(BF16)
+            return 0
+
+        lax.fori_loop(0, HEADS // 4, four, 0)
+
+    renew(0, k_buf)
+    store_keys = pltpu.make_async_copy(k_buf, out_keys, store_sem.at[0])
+    store_keys.start()
 
     received(wu_g.at[pl.ds(0, 3)], 6)
     across(wu_g, 7, False)
     received(wd_g.at[pl.ds(0, 3)], 8)
     across(wd_g, 9, False)
-    renew(1, v_buf)
-    store_values = pltpu.make_async_copy(v_buf, out_values, store_sem.at[1])
-    store_values.start()
-
     received(a_g.at[pl.ds(0, SEQ - 1)], 12)
     total = jnp.zeros((ROWS, 128), F32)
     for k in range(REQ):
@@ -363,6 +404,9 @@
     total += jnp.concatenate([bo_s[...], bo_s[...]], axis=1)
     o_g[s] = jnp.where(low, total[:16], total[16:]).astype(BF16)
     spread(o_g.at[s], o_g, 13)
+    renew(1, v_buf)
+    store_values = pltpu.make_async_copy(v_buf, out_values, store_sem.at[1])
+    store_values.start()
     received(wu_g.at[pl.ds(0, 4)], 7)
     received(wd_g.at[pl.ds(0, 4)], 9)
     received(o_g.at[pl.ds(0, SEQ - 1)], 13)
@@ -403,8 +447,10 @@
     for buf, phase in ((wq_g, 0), (wkvo_g, 2), (wu_g, 6), (wd_g, 8)):
         sent(buf.at[pl.ds(0, 3)], phase)
         sent(buf.at[pl.ds(0, 4)], phase + 1)
-    for buf, phase in ((q_g, 4), (kv_g, 5), (p_g, 10), (t_g, 11), (a_g, 12), (o_g, 13), (f_g, 14)):
+    for buf, phase in ((q_g, 4), (p_g, 10), (a_g, 12), (o_g, 13), (f_g, 14)):
         sent(buf.at[pl.ds(0, SEQ - 1)], phase)
+    sent(kv_g.at[pl.ds(0, SEQ - 2)], 5)
+    sent(kv_g.at[0], 11)
     received(h_g.at[pl.ds(0, SEQ - 1)], 15)
     for j in range(HEADS):
         whole = jnp.concatenate([h_g[2 * j], h_g[2 * j + 1]], axis=0).astype(F32)
@@ -492,10 +538,8 @@
             pltpu.VMEM((REQ, 256, 256), BF16),
             slots,
             pltpu.VMEM((SEQ, 2, 16, 128), BF16),
-            slots,
-            slots,
-            pltpu.VMEM((HEADS, 1, 128), F32),
-            pltpu.VMEM((SEQ, 1, 128), F32),
+            pltpu.VMEM((SEQ, 32, 128), BF16),
+            pltpu.VMEM((SEQ, 32, 128), BF16),
             slots,
             slots,
             slots,
@@ -505,6 +549,9 @@
             pltpu.SemaphoreType.DMA((2,)),
             pltpu.SemaphoreType.DMA((16,)),
             pltpu.SemaphoreType.DMA((16,)),
+            pltpu.SemaphoreType.DMA((SEQ,)),
+            pltpu.SemaphoreType.REGULAR,
+            pltpu.SemaphoreType.REGULAR,
         ],
         compiler_params=pltpu.CompilerParams(
             collective_id=0, has_side_effects=True, vmem_limit_bytes=58 * 1024 * 1024

time: 66 us -> 64.2 us (0.973)
  Pallas kernels: 65.3 us -> 63.5 us
    pallas_call x1, Pallas kernels: 61.8 us -> 60 us  [body(): pl.pallas_call(kernel, out_shape=(jax.ShapeDtypeStruct((8, 4, WIDTH), BF1...]
where the time goes in v3:
time: 64.2 us
  Pallas kernels  63.5 us (99%)
  between operations  0.65 us (1%)
    pallas_call x1, Pallas kernels, body(): pl.pallas_call(kernel, out_shape=(jax.ShapeDtypeStruct((8, 4, WIDTH), BF1...  60 us
    pallas_call x1, Pallas kernels, body(): pl.pallas_call(finish, out_shape=(jax.ShapeDtypeStruct((8, 4, WIDTH), BF1...  3.5 us

profile of v3, /device:TPU:2, one launch (start us, length us, event | category | flops | bytes accessed | tf_op | source)
XLA Modules:
  0.0 64.2 jit_solution(8591767797823639038)
XLA Ops:
  0.6 60.0 %shard_map.211 = (bf16[8,4,2048]{2,1,0:T(4,128)(2,1)}, bf16[512,2048]{1,0:T(8,128)(2,1)}, bf16[512,2048]{1,0:T(8,128)(2,1)}) custom-call(s32[8]{0:T(128)} %lengths.1, bf16[8,4,2048]{2,1,0:T(4,128)(2,1)} %tokens.1, bf16[512,2048]{1,0:T(8,128)(2,1)} %bitcast.18, bf16[512,2048]{1,0:T(8,128)(2,1)} %bitcast.19, f32[1,2048]{1,0:T(1,128)} %bitcast.24, ...), custom_call_target="tpu_custom_call" | custom-call | flops 500000000 | bytes 9000000 | tf_op jit(solution)/shard_map/pallas_call | solution.py:509
  60.7 3.5 %shard_map.212 = (bf16[8,4,2048]{2,1,0:T(4,128)(2,1)}, bf16[512,2048]{1,0:T(8,128)(2,1)}, bf16[512,2048]{1,0:T(8,128)(2,1)}) custom-call(bf16[8,4,2048]{2,1,0:T(4,128)(2,1)} %get-tuple-element.9.hidden, bf16[512,2048]{1,0:T(8,128)(2,1)} %get-tuple-element.10.keys, bf16[512,2048]{1,0:T(8,128)(2,1)} %get-tuple-element.11.values), custom_call_target="tpu_custom_call" | custom-call | tf_op jit(solution)/shard_map/pallas_call | solution.py:582

commit v4 on v3

--- a/solution.py
+++ b/solution.py
@@ -40,8 +40,11 @@
 
 
 def unfold(slots, j):
-    first = slots[2 * j].astype(F32)
-    second = slots[2 * j + 1].astype(F32)
+    return unfold_pair(slots[2 * j], slots[2 * j + 1])
+
+
+def unfold_pair(first, second):
+    first, second = first.astype(F32), second.astype(F32)
     low = lax.broadcasted_iota(jnp.int32, (16, 128), 1) < 64
     top = jnp.where(low, first, pltpu.roll(second, 64, 1))
     bottom = jnp.where(low, pltpu.roll(first, 64, 1), second)
@@ -94,6 +97,7 @@
     wd_g,
     q_g,
     kv_g,
+    kv_p,
     p_s,
     p_g,
     a_g,
@@ -245,6 +249,11 @@
     across(wkvo_g, 3, False)
     for load in loads[12:]:
         load.wait()
+
+    along_y(wu_g, 6)
+    across(wu_g, 7, True)
+    along_y(wd_g, 8)
+    across(wd_g, 9, True)
 
     scale = HEAD**-0.5
     row = lax.broadcasted_iota(jnp.int32, (ROWS, SPOTS), 0)
@@ -303,34 +312,20 @@
             preferred_element_type=F32,
         )
     total += jnp.concatenate([bk_s[...], bv_s[...]], axis=1)
-    kv_g[s, 0] = jnp.where(low, total[:16], pltpu.roll(total[16:], 64, 1)).astype(BF16)
-    kv_g[s, 1] = jnp.where(low, pltpu.roll(total[:16], 64, 1), total[16:]).astype(BF16)
-    send(kv_g.at[s], kv_g.at[s], 11, (partner, r))
-
-    def share_rows(i, _):
-        peer = far(i)
-
-        @pl.when(peer != partner)
-        def _():
-            send(kv_g.at[s], kv_g.at[s], 5, (peer, r))
-
-        return 0
-
-    lax.fori_loop(0, SEQ - 1, share_rows, 0)
-
-    along_y(wu_g, 6)
-    across(wu_g, 7, True)
-    along_y(wd_g, 8)
-    across(wd_g, 9, True)
-
-    def mine(slots):
-        return unfold(slots, head)
-
-    received(kv_g.at[0], 11)
-    query = mine(q_g)
+    kv_g[x, z, 0] = jnp.where(low, total[:16], pltpu.roll(total[16:], 64, 1)).astype(BF16)
+    kv_g[x, z, 1] = jnp.where(low, pltpu.roll(total[:16], 64, 1), total[16:]).astype(BF16)
+    send(kv_g.at[x, z], kv_p, 11, (partner, r))
+
+    def mine(which):
+        own, other = kv_g[x, z, which].astype(F32), kv_p[which].astype(F32)
+        first, second = jnp.where(half == 0, own, other), jnp.where(half == 0, other, own)
+        return unfold_pair(first, second).astype(BF16)
+
+    received(kv_p, 11)
+    query = unfold(q_g, head)
     query = jnp.where(half == 0, query[:16], query[16:]).astype(BF16)
-    fresh_keys = mine(kv_g.at[:, 0]).astype(BF16)
-    fresh_values = mine(kv_g.at[:, 1]).astype(BF16)
+    fresh_keys = mine(0)
+    fresh_values = mine(1)
     row = lax.broadcasted_iota(jnp.int32, (16, ROWS), 0) + half * 16
     col = lax.broadcasted_iota(jnp.int32, (16, ROWS), 1)
     scores = lax.dot_general(query, fresh_keys, NT, preferred_element_type=F32) * scale
@@ -358,32 +353,8 @@
     a_g[s] = (mixed / total).astype(BF16)
     spread(a_g.at[s], a_g, 12)
 
-    received(kv_g.at[pl.ds(0, SEQ - 2)], 5)
-    spot = lax.broadcasted_iota(jnp.int32, (SPOTS, ROWS), 0)
-    new = lax.broadcasted_iota(jnp.int32, (SPOTS, ROWS), 1)
-    start = jnp.zeros((SPOTS, ROWS), jnp.int32)
-    for k in range(8):
-        start = jnp.where((new >> 2) == k, lengths_s[k], start)
-    hit = ((new >> 2) == (spot >> 6)) & ((spot & 63) + s * 64 == start + (new & 3))
-    pick = jnp.where(hit, 1.0, 0.0)
-    changed = jnp.max(pick, axis=1, keepdims=True) > 0.5
-    pick = pick.astype(BF16)
-
-    def renew(which, buf):
-        def four(g, _):
-            columns = [pl.ds(pl.multiple_of((4 * g + j) * 128, 128), 128) for j in range(4)]
-            rows = [unfold(kv_g.at[:, which], 4 * g + j).astype(BF16) for j in range(4)]
-            fresh = [jnp.dot(pick, row, preferred_element_type=F32) for row in rows]
-            for j in range(4):
-                old = buf[:, columns[j]].astype(F32)
-                buf[:, columns[j]] = jnp.where(changed, fresh[j], old).astype(BF16)
-            return 0
-
-        lax.fori_loop(0, HEADS // 4, four, 0)
-
-    renew(0, k_buf)
-    store_keys = pltpu.make_async_copy(k_buf, out_keys, store_sem.at[0])
-    store_keys.start()
+    for dz in (4, 3, 5, 2, 6, 1, 7):
+        send(kv_g.at[x, z], kv_g.at[x, z], 5, along(dz, 0))
 
     received(wu_g.at[pl.ds(0, 3)], 6)
     across(wu_g, 7, False)
@@ -404,9 +375,10 @@
     total += jnp.concatenate([bo_s[...], bo_s[...]], axis=1)
     o_g[s] = jnp.where(low, total[:16], total[16:]).astype(BF16)
     spread(o_g.at[s], o_g, 13)
-    renew(1, v_buf)
-    store_values = pltpu.make_async_copy(v_buf, out_values, store_sem.at[1])
-    store_values.start()
+    received(kv_g.at[0, pl.ds(0, 7)], 5)
+    for dx in (2, 1, 3):
+        send(kv_g.at[x], kv_g.at[x], 16, along(0, dx))
+
     received(wu_g.at[pl.ds(0, 4)], 7)
     received(wd_g.at[pl.ds(0, 4)], 9)
     received(o_g.at[pl.ds(0, SEQ - 1)], 13)
@@ -433,6 +405,39 @@
 
     lax.fori_loop(0, SEQ - 1, scatter, 0)
     f_g[s] = f_s[s]
+
+    received(kv_g.at[pl.ds(0, 3)], 16)
+    spot = lax.broadcasted_iota(jnp.int32, (SPOTS, ROWS), 0)
+    new = lax.broadcasted_iota(jnp.int32, (SPOTS, ROWS), 1)
+    start = jnp.zeros((SPOTS, ROWS), jnp.int32)
+    for k in range(8):
+        start = jnp.where((new >> 2) == k, lengths_s[k], start)
+    hit = ((new >> 2) == (spot >> 6)) & ((spot & 63) + s * 64 == start + (new & 3))
+    pick = jnp.where(hit, 1.0, 0.0)
+    changed = jnp.max(pick, axis=1, keepdims=True) > 0.5
+    pick = pick.astype(BF16)
+
+    def renew(which, buf):
+        def four(g, _):
+            columns = [pl.ds(pl.multiple_of((4 * g + j) * 128, 128), 128) for j in range(4)]
+            rows = [
+                unfold_pair(
+                    kv_g[2 * (j % 2), 2 * g + j // 2, which], kv_g[2 * (j % 2) + 1, 2 * g + j // 2, which]
+                ).astype(BF16)
+                for j in range(4)
+            ]
+            fresh = [jnp.dot(pick, row, preferred_element_type=F32) for row in rows]
+            for j in range(4):
+                old = buf[:, columns[j]].astype(F32)
+                buf[:, columns[j]] = jnp.where(changed, fresh[j], old).astype(BF16)
+            return 0
+
+        lax.fori_loop(0, HEADS // 4, four, 0)
+
+    renew(0, k_buf)
+    store_keys = pltpu.make_async_copy(k_buf, out_keys, store_sem.at[0])
+    store_keys.start()
+
     columns = pl.ds(pl.multiple_of(head * 128, 128), 128)
     mid = x_buf[pl.ds(pl.multiple_of(half * 16, 16), 16), columns] + bd_s[:, columns]
     received(f_g.at[pl.ds(0, SEQ - 1)], 14)
@@ -441,22 +446,26 @@
         summed += f_g[k].astype(F32)
     h_g[s] = (mid + summed).astype(BF16)
     spread(h_g.at[s], h_g, 15)
-
-    store_keys.wait()
-    store_values.wait()
+    renew(1, v_buf)
+    store_values = pltpu.make_async_copy(v_buf, out_values, store_sem.at[1])
+    store_values.start()
+
     for buf, phase in ((wq_g, 0), (wkvo_g, 2), (wu_g, 6), (wd_g, 8)):
         sent(buf.at[pl.ds(0, 3)], phase)
         sent(buf.at[pl.ds(0, 4)], phase + 1)
     for buf, phase in ((q_g, 4), (p_g, 10), (a_g, 12), (o_g, 13), (f_g, 14)):
         sent(buf.at[pl.ds(0, SEQ - 1)], phase)
-    sent(kv_g.at[pl.ds(0, SEQ - 2)], 5)
-    sent(kv_g.at[0], 11)
+    sent(kv_g.at[0, pl.ds(0, 7)], 5)
+    sent(kv_g.at[pl.ds(0, 3)], 16)
+    sent(kv_p, 11)
     received(h_g.at[pl.ds(0, SEQ - 1)], 15)
     for j in range(HEADS):
         whole = jnp.concatenate([h_g[2 * j], h_g[2 * j + 1]], axis=0).astype(F32)
         for i in range(8):
             out[i, :, 128 * j : 128 * j + 128] = whole[4 * i : 4 * i + 4].astype(BF16)
     sent(h_g.at[pl.ds(0, SEQ - 1)], 15)
+    store_keys.wait()
+    store_values.wait()
 
 
 def finish(hidden, keys, values, out, out_keys, out_values, h_buf, k_buf, v_buf, in_sem, out_sem):
@@ -537,7 +546,8 @@
             pltpu.VMEM((REQ, 256, 256), BF16),
             pltpu.VMEM((REQ, 256, 256), BF16),
             slots,
-            pltpu.VMEM((SEQ, 2, 16, 128), BF16),
+            pltpu.VMEM((4, 8, 2, 16, 128), BF16),
+            pltpu.VMEM((2, 16, 128), BF16),
             pltpu.VMEM((SEQ, 32, 128), BF16),
             pltpu.VMEM((SEQ, 32, 128), BF16),
             slots,
@@ -547,8 +557,8 @@
             slots,
             pltpu.SemaphoreType.DMA((20,)),
             pltpu.SemaphoreType.DMA((2,)),
-            pltpu.SemaphoreType.DMA((16,)),
-            pltpu.SemaphoreType.DMA((16,)),
+            pltpu.SemaphoreType.DMA((17,)),
+            pltpu.SemaphoreType.DMA((17,)),
             pltpu.SemaphoreType.DMA((SEQ,)),
             pltpu.SemaphoreType.REGULAR,
             pltpu.SemaphoreType.REGULAR,

time: 64.2 us -> 62.5 us (0.974)
  Pallas kernels: 63.5 us -> 61.8 us
    pallas_call x1, Pallas kernels: 60 us -> 58.3 us  [body(): pl.pallas_call(kernel, out_shape=(jax.ShapeDtypeStruct((8, 4, WIDTH), BF1...]
where the time goes in v4:
time: 62.5 us; the launch traced here: 62.4 us
  Pallas kernels  61.8 us (99%)
  between operations  0.65 us (1%)
    pallas_call x1, Pallas kernels, body(): pl.pallas_call(kernel, out_shape=(jax.ShapeDtypeStruct((8, 4, WIDTH), BF1...  58.3 us
    pallas_call x1, Pallas kernels, body(): pl.pallas_call(finish, out_shape=(jax.ShapeDtypeStruct((8, 4, WIDTH), BF1...  3.5 us

profile of v4, /device:TPU:2, one launch (start us, length us, event | category | flops | bytes accessed | tf_op | source)
XLA Modules:
  0.0 62.4 jit_solution(14105373591108125540)
XLA Ops:
  0.6 58.3 %shard_map.211 = (bf16[8,4,2048]{2,1,0:T(4,128)(2,1)}, bf16[512,2048]{1,0:T(8,128)(2,1)}, bf16[512,2048]{1,0:T(8,128)(2,1)}) custom-call(s32[8]{0:T(128)} %lengths.1, bf16[8,4,2048]{2,1,0:T(4,128)(2,1)} %tokens.1, bf16[512,2048]{1,0:T(8,128)(2,1)} %bitcast.18, bf16[512,2048]{1,0:T(8,128)(2,1)} %bitcast.19, f32[1,2048]{1,0:T(1,128)} %bitcast.24, ...), custom_call_target="tpu_custom_call" | custom-call | flops 500000000 | bytes 9000000 | tf_op jit(solution)/shard_map/pallas_call | solution.py:518
  58.9 3.5 %shard_map.212 = (bf16[8,4,2048]{2,1,0:T(4,128)(2,1)}, bf16[512,2048]{1,0:T(8,128)(2,1)}, bf16[512,2048]{1,0:T(8,128)(2,1)}) custom-call(bf16[8,4,2048]{2,1,0:T(4,128)(2,1)} %get-tuple-element.9.hidden, bf16[512,2048]{1,0:T(8,128)(2,1)} %get-tuple-element.10.keys, bf16[512,2048]{1,0:T(8,128)(2,1)} %get-tuple-element.11.values), custom_call_target="tpu_custom_call" | custom-call | tf_op jit(solution)/shard_map/pallas_call | solution.py:592

commit v5 on v4

--- a/solution.py
+++ b/solution.py
@@ -32,11 +32,12 @@
     return center * lax.rsqrt(spread + 1e-05) * gain + shift
 
 
-def far_first(i):
-    a, b = i // 4, lax.rem(i, 4)
-    dz = 4 + ((a + 1) // 2) * (1 - 2 * lax.rem(a, 2))
-    dx = 2 + ((b + 1) // 2) * (1 - 2 * lax.rem(b, 2))
-    return dz, dx
+def hops(offset):
+    dz, dx = offset
+    return min(dz, 8 - dz) + min(dx, 4 - dx)
+
+
+FAR = sorted(((dz, dx) for dz in range(8) for dx in range(4) if dz + dx), key=hops, reverse=True)
 
 
 def unfold(slots, j):
@@ -123,12 +124,8 @@
 
     barrier = pltpu.get_barrier_semaphore()
 
-    def far(i):
-        dz, dx = far_first(i)
-        return lax.rem(z + dz, 8) * 4 + lax.rem(x + dx, 4)
-
     def along(dz, dx):
-        return (lax.rem(z + dz, 8) * 4 + lax.rem(x + dx, 4), r)
+        return (((z + dz) & 7) * 4 + ((x + dx) & 3), r)
 
     for dz, dx in ((2, 0), (6, 0), (0, 2), (1, 0), (7, 0), (0, 1), (0, 3)):
         pl.semaphore_signal(barrier, inc=1, device_id=along(dz, dx), device_id_type=MESH)
@@ -184,11 +181,8 @@
         ).wait_send()
 
     def spread(src, slots, phase):
-        def one(i, _):
-            send(src, slots.at[s], phase, (far(i), r))
-            return 0
-
-        lax.fori_loop(0, SEQ - 1, one, 0)
+        for offset in FAR:
+            send(src, slots.at[s], phase, along(*offset))
 
     def along_y(buf, phase):
         for k in (2, 1, 3):
@@ -232,18 +226,15 @@
 
     pl.semaphore_wait(plane_sem, 3)
 
-    def share_queries(i, _):
+    for offset in FAR:
         pltpu.make_async_remote_copy(
             q_g.at[s],
             q_g.at[s],
             send_sem.at[4],
             query_sem.at[s],
-            device_id=(far(i), r),
+            device_id=along(*offset),
             device_id_type=MESH,
         ).start()
-        return 0
-
-    lax.fori_loop(0, SEQ - 1, share_queries, 0)
 
     received(wkvo_g.at[pl.ds(0, 3)], 2)
     across(wkvo_g, 3, False)
@@ -398,12 +389,9 @@
         f_s[4 * k + 2] = feed[:16, 128:]
         f_s[4 * k + 3] = feed[16:, 128:]
 
-    def scatter(i, _):
-        peer = far(i)
-        send(f_s.at[peer], f_g.at[s], 14, (peer, r))
-        return 0
-
-    lax.fori_loop(0, SEQ - 1, scatter, 0)
+    for offset in FAR:
+        peer = along(*offset)
+        send(f_s.at[peer[0]], f_g.at[s], 14, peer)
     f_g[s] = f_s[s]
 
     received(kv_g.at[pl.ds(0, 3)], 16)

time: 62.5 us -> 61.8 us (0.989)
  Pallas kernels: 61.8 us -> 61.1 us
    pallas_call x1, Pallas kernels: 58.3 us -> 57.6 us  [body(): pl.pallas_call(kernel, out_shape=(jax.ShapeDtypeStruct((8, 4, WIDTH), BF1...]
where the time goes in v5:
time: 61.8 us; the launch traced here: 61.7 us
  Pallas kernels  61.1 us (99%)
  between operations  0.65 us (1%)
    pallas_call x1, Pallas kernels, body(): pl.pallas_call(kernel, out_shape=(jax.ShapeDtypeStruct((8, 4, WIDTH), BF1...  57.6 us
    pallas_call x1, Pallas kernels, body(): pl.pallas_call(finish, out_shape=(jax.ShapeDtypeStruct((8, 4, WIDTH), BF1...  3.5 us

profile of v5, /device:TPU:2, one launch (start us, length us, event | category | flops | bytes accessed | tf_op | source)
XLA Modules:
  0.0 61.7 jit_solution(2262184027224122469)
XLA Ops:
  0.6 57.6 %shard_map.211 = (bf16[8,4,2048]{2,1,0:T(4,128)(2,1)}, bf16[512,2048]{1,0:T(8,128)(2,1)}, bf16[512,2048]{1,0:T(8,128)(2,1)}) custom-call(s32[8]{0:T(128)} %lengths.1, bf16[8,4,2048]{2,1,0:T(4,128)(2,1)} %tokens.1, bf16[512,2048]{1,0:T(8,128)(2,1)} %bitcast.18, bf16[512,2048]{1,0:T(8,128)(2,1)} %bitcast.19, f32[1,2048]{1,0:T(1,128)} %bitcast.24, ...), custom_call_target="tpu_custom_call" | custom-call | flops 500000000 | bytes 9000000 | tf_op jit(solution)/shard_map/pallas_call | solution.py:506
  58.2 3.5 %shard_map.212 = (bf16[8,4,2048]{2,1,0:T(4,128)(2,1)}, bf16[512,2048]{1,0:T(8,128)(2,1)}, bf16[512,2048]{1,0:T(8,128)(2,1)}) custom-call(bf16[8,4,2048]{2,1,0:T(4,128)(2,1)} %get-tuple-element.9.hidden, bf16[512,2048]{1,0:T(8,128)(2,1)} %get-tuple-element.10.keys, bf16[512,2048]{1,0:T(8,128)(2,1)} %get-tuple-element.11.values), custom_call_target="tpu_custom_call" | custom-call | tf_op jit(solution)/shard_map/pallas_call | solution.py:580

commit v6 on v5

--- a/solution.py
+++ b/solution.py
@@ -447,29 +447,36 @@
     sent(kv_g.at[pl.ds(0, 3)], 16)
     sent(kv_p, 11)
     received(h_g.at[pl.ds(0, SEQ - 1)], 15)
-    for j in range(HEADS):
-        whole = jnp.concatenate([h_g[2 * j], h_g[2 * j + 1]], axis=0).astype(F32)
-        for i in range(8):
-            out[i, :, 128 * j : 128 * j + 128] = whole[4 * i : 4 * i + 4].astype(BF16)
+    out[...] = h_g[...]
     sent(h_g.at[pl.ds(0, SEQ - 1)], 15)
     store_keys.wait()
     store_values.wait()
 
 
-def finish(hidden, keys, values, out, out_keys, out_values, h_buf, k_buf, v_buf, in_sem, out_sem):
+def finish(hidden, keys, values, out, out_keys, out_values, h_g, h_buf, k_buf, v_buf, in_sem, out_sem):
     half = SPOTS // 2
-    moves = [(hidden, h_buf, out)]
+    moves = []
     for a, b, c in ((keys, k_buf, out_keys), (values, v_buf, out_values)):
         for i in range(2):
             part = pl.ds(i * half, half)
             moves.append((a.at[part], b.at[part], c.at[part]))
+    arrive = pltpu.make_async_copy(hidden, h_g, in_sem.at[4])
+    leave = pltpu.make_async_copy(h_buf, out, out_sem.at[4])
+    arrive.start()
     ins = [pltpu.make_async_copy(a, b, in_sem.at[i]) for i, (a, b, _) in enumerate(moves)]
     outs = [pltpu.make_async_copy(b, c, out_sem.at[i]) for i, (_, b, c) in enumerate(moves)]
     for copy in ins:
         copy.start()
+    arrive.wait()
+    for j in range(HEADS):
+        whole = jnp.concatenate([h_g[2 * j], h_g[2 * j + 1]], axis=0).astype(F32)
+        for i in range(8):
+            h_buf[i, :, 128 * j : 128 * j + 128] = whole[4 * i : 4 * i + 4].astype(BF16)
+    leave.start()
     for arrived, copy in zip(ins, outs):
         arrived.wait()
         copy.start()
+    leave.wait()
     for copy in outs:
         copy.wait()
 
@@ -506,7 +513,7 @@
     hidden_out, new_keys, new_values = pl.pallas_call(
         kernel,
         out_shape=(
-            jax.ShapeDtypeStruct((8, 4, WIDTH), BF16),
+            jax.ShapeDtypeStruct((SEQ, 16, 128), BF16),
             jax.ShapeDtypeStruct((SPOTS, WIDTH), BF16),
             jax.ShapeDtypeStruct((SPOTS, WIDTH), BF16),
         ),
@@ -587,6 +594,7 @@
         in_specs=[hbm] * 3,
         out_specs=(hbm, hbm, hbm),
         scratch_shapes=[
+            pltpu.VMEM((SEQ, 16, 128), BF16),
             pltpu.VMEM((8, 4, WIDTH), BF16),
             pltpu.VMEM((SPOTS, WIDTH), BF16),
             pltpu.VMEM((SPOTS, WIDTH), BF16),

time: 61.8 us -> 61.8 us (level)
  no operation moved by 1% of the time
where the time goes in v6:
time: 61.8 us; the launch traced here: 61.7 us
  Pallas kernels  61.1 us (99%)
  between operations  0.65 us (1%)
    pallas_call x1, Pallas kernels, body(): pl.pallas_call(kernel, out_shape=(jax.ShapeDtypeStruct((SEQ, 16, 128), BF...  57.6 us
    pallas_call x1, Pallas kernels, body(): pl.pallas_call(finish, out_shape=(jax.ShapeDtypeStruct((8, 4, WIDTH), BF1...  3.5 us

profile of v6, /device:TPU:2, one launch (start us, length us, event | category | flops | bytes accessed | tf_op | source)
XLA Modules:
  0.0 61.7 jit_solution(15661449882458998527)
XLA Ops:
  0.6 57.6 %shard_map.211 = (bf16[32,16,128]{2,1,0:T(8,128)(2,1)}, bf16[512,2048]{1,0:T(8,128)(2,1)}, bf16[512,2048]{1,0:T(8,128)(2,1)}) custom-call(s32[8]{0:T(128)} %lengths.1, bf16[8,4,2048]{2,1,0:T(4,128)(2,1)} %tokens.1, bf16[512,2048]{1,0:T(8,128)(2,1)} %bitcast.18, bf16[512,2048]{1,0:T(8,128)(2,1)} %bitcast.19, f32[1,2048]{1,0:T(1,128)} %bitcast.24, ...), custom_call_target="tpu_custom_call" | custom-call | flops 500000000 | bytes 9000000 | tf_op jit(solution)/shard_map/pallas_call | solution.py:513
  58.2 3.5 %shard_map.212 = (bf16[8,4,2048]{2,1,0:T(4,128)(2,1)}, bf16[512,2048]{1,0:T(8,128)(2,1)}, bf16[512,2048]{1,0:T(8,128)(2,1)}) custom-call(bf16[32,16,128]{2,1,0:T(8,128)(2,1)} %get-tuple-element.9.hidden, bf16[512,2048]{1,0:T(8,128)(2,1)} %get-tuple-element.10.keys, bf16[512,2048]{1,0:T(8,128)(2,1)} %get-tuple-element.11.values), custom_call_target="tpu_custom_call" | custom-call | tf_op jit(solution)/shard_map/pallas_call | solution.py:587
